TPU v7x, 256 devices: a whole 4x4x8 slice. The times are simulated.
256 devices in a mesh: pipe: 8 (over z_hi, core), dp: 32 (over z_lo, y, x).
Axes of the slice: x: 4, y: 4, z: 8 (z_hi: 4, z_lo: 2; z = z_hi * 2 + z_lo), core: 2. Of those that a mesh axis runs over, the one named last changes fastest.
Arguments:
- item_ids: int32 [4, 1056], P(None, 'dp'), may hold values from 0 to 127
- plan_order: int32 [4], replicated, may hold values from 0 to 3, each once
- candidates: bfloat16 [128, 3072], replicated, may hold values from -6 to 6
- adapters_in: bfloat16 [8, 2, 3072, 256], P('pipe'), may hold values from -0.109375 to 0.109375
- adapters_out: bfloat16 [8, 2, 256, 3072], P('pipe'), may hold values from -0.1875 to 0.1875
Outputs:
- grad_in: float32 [8, 2, 3072, 256], P('pipe', None, 'dp')
- grad_out: float32 [8, 2, 256, 3072], P('pipe', None, None, 'dp')
Inputs may be any that keep to these rules, and one draw needn't show every extreme that they name: `plan_order`: a permutation of the micro-batches.
All inputs are finite; a program needn't handle non-finite values.
Results may differ from a plain program's by a relative error of at most 0.025.
Values may be sent and summed in bfloat16 or wider, within the bound.
A program may use at most 128 MiB of HBM per device.

v0:
```python
import math

import jax
import jax.numpy as jnp
from jax import lax
from jax.sharding import PartitionSpec as P


def from_behind(x, axis, by):
    length = lax.axis_size(axis)
    pairs = [(i, i + by) for i in range(length) if 0 <= i + by < length]
    return lax.ppermute(x, axis, pairs)


def advance(inputs, w_first, w_second):
    pre_act = jnp.dot(inputs, w_first, preferred_element_type=jnp.float32)
    activated = jax.nn.silu(pre_act).astype(jnp.bfloat16)
    branch = jnp.dot(activated, w_second, preferred_element_type=jnp.float32)
    return ((inputs.astype(jnp.float32) + branch).astype(jnp.bfloat16), pre_act)


def retreat(pre_act, w_first, w_second, grad_y):
    logistic = jax.nn.sigmoid(pre_act)
    slope = logistic * (1.0 + pre_act * (1.0 - logistic))
    grad_act = jnp.einsum("rd,hd->rh", grad_y, w_second, preferred_element_type=jnp.float32)
    grad_pre = (grad_act * slope).astype(jnp.bfloat16)
    back_term = jnp.einsum("rh,dh->rd", grad_pre, w_first, preferred_element_type=jnp.float32)
    grad_x = (grad_y.astype(jnp.float32) + back_term).astype(jnp.bfloat16)
    activated = jax.nn.silu(pre_act).astype(jnp.bfloat16)
    return (grad_x, grad_pre, activated)


def place_item(buffer, fresh_value, slot_index, is_live):
    previous = lax.dynamic_index_in_dim(buffer, slot_index, 0, keepdims=False)
    return lax.dynamic_update_index_in_dim(
        buffer, jnp.where(is_live, fresh_value, previous), slot_index, 0
    )


def local(item_ids, plan_order, candidates, adapters_in, adapters_out):
    sections = lax.axis_size("pipe")
    workers = lax.axis_size("dp")
    position = lax.axis_index("pipe")
    batches = item_ids.shape[0]
    half_count = batches // 2
    events = item_ids.shape[1] - 1
    features = candidates.shape[1]
    hidden = adapters_in.shape[3]
    last_section = sections - 1
    clock_count = half_count + sections - 1
    scale = 1.0 / math.sqrt(batches * workers * events)
    numbers = jnp.arange(batches, dtype=jnp.int32)
    slot_of = jnp.sum(
        jnp.where(plan_order[None, :] == numbers[:, None], numbers[None, :], 0), axis=1
    )
    arranged = jnp.take(item_ids, slot_of, axis=0)
    catalog = jnp.arange(candidates.shape[0], dtype=jnp.int32)

    def lookup(chosen):
        one_hot = (chosen[..., None] == catalog).astype(jnp.bfloat16)
        return jnp.einsum("mec,cd->med", one_hot, candidates, preferred_element_type=jnp.float32)

    embedded = lookup(arranged[:, :events]).astype(jnp.bfloat16)
    seed_grads = (lookup(arranged[:, 1:]) * scale).astype(jnp.bfloat16)
    first_in = adapters_in[0, 0]
    first_out = adapters_out[0, 0]
    second_in = adapters_in[0, 1]
    second_out = adapters_out[0, 1]
    blank_rows = jnp.zeros((events, features), jnp.bfloat16)
    blank_items = jnp.zeros((half_count, events, features), jnp.bfloat16)
    blank_pre = jnp.zeros((half_count, events, hidden), jnp.float32)
    blank_small = jnp.zeros((half_count, events, hidden), jnp.bfloat16)

    def empty_stash():
        return (blank_items, blank_pre)

    def forward_phase(fresh_up, fresh_down):

        def forward_clock_step(moment, loop_state):
            recv_up, recv_down, stash_up, stash_down, ends_up, ends_down = loop_state
            item_up = moment - position
            item_down = moment - (last_section - position)
            slot_up = jnp.clip(item_up, 0, half_count - 1)
            slot_down = jnp.clip(item_down, 0, half_count - 1)
            live_up = (item_up >= 0) & (item_up < half_count)
            live_down = (item_down >= 0) & (item_down < half_count)
            input_up = jnp.where(
                position == 0,
                lax.dynamic_index_in_dim(fresh_up, slot_up, 0, keepdims=False),
                recv_up,
            )
            input_down = jnp.where(
                position == last_section,
                lax.dynamic_index_in_dim(fresh_down, slot_down, 0, keepdims=False),
                recv_down,
            )
            output_up, pre_up = advance(input_up, first_in, first_out)
            output_down, pre_down = advance(input_down, second_in, second_out)
            stash_up = (
                place_item(stash_up[0], input_up, slot_up, live_up),
                place_item(stash_up[1], pre_up, slot_up, live_up),
            )
            stash_down = (
                place_item(stash_down[0], input_down, slot_down, live_down),
                place_item(stash_down[1], pre_down, slot_down, live_down),
            )
            ends_up = place_item(ends_up, output_up, slot_up, live_up)
            ends_down = place_item(ends_down, output_down, slot_down, live_down)
            recv_up = from_behind(output_up, "pipe", 1)
            recv_down = from_behind(output_down, "pipe", -1)
            return (recv_up, recv_down, stash_up, stash_down, ends_up, ends_down)

        start_state = (
            blank_rows,
            blank_rows,
            empty_stash(),
            empty_stash(),
            blank_items,
            blank_items,
        )
        return lax.fori_loop(0, clock_count, forward_clock_step, start_state)

    def backward_phase(seed_down, seed_up, stash_down, stash_up):

        def pre_of(stash, slot_index):
            return lax.dynamic_index_in_dim(stash[1], slot_index, 0, keepdims=False)

        def backward_clock_step(moment, loop_state):
            recv_down, recv_up, grads_down, grads_up, ends_down, ends_up = loop_state
            item_down = moment - position
            item_up = moment - (last_section - position)
            slot_down = jnp.clip(item_down, 0, half_count - 1)
            slot_up = jnp.clip(item_up, 0, half_count - 1)
            live_down = (item_down >= 0) & (item_down < half_count)
            live_up = (item_up >= 0) & (item_up < half_count)
            grad_down = jnp.where(
                position == 0,
                lax.dynamic_index_in_dim(seed_down, slot_down, 0, keepdims=False),
                recv_down,
            )
            grad_up = jnp.where(
                position == last_section,
                lax.dynamic_index_in_dim(seed_up, slot_up, 0, keepdims=False),
                recv_up,
            )
            back_down, pre_grad_down, act_down = retreat(
                pre_of(stash_down, slot_down), second_in, second_out, grad_down
            )
            back_up, pre_grad_up, act_up = retreat(
                pre_of(stash_up, slot_up), first_in, first_out, grad_up
            )
            grads_down = (
                place_item(grads_down[0], grad_down, slot_down, live_down),
                place_item(grads_down[1], pre_grad_down, slot_down, live_down),
                place_item(grads_down[2], act_down, slot_down, live_down),
            )
            grads_up = (
                place_item(grads_up[0], grad_up, slot_up, live_up),
                place_item(grads_up[1], pre_grad_up, slot_up, live_up),
                place_item(grads_up[2], act_up, slot_up, live_up),
            )
            ends_down = place_item(ends_down, back_down, slot_down, live_down)
            ends_up = place_item(ends_up, back_up, slot_up, live_up)
            recv_down = from_behind(back_down, "pipe", 1)
            recv_up = from_behind(back_up, "pipe", -1)
            return (recv_down, recv_up, grads_down, grads_up, ends_down, ends_up)

        empty_grads = (blank_items, blank_small, blank_small)
        start_state = (blank_rows, blank_rows, empty_grads, empty_grads, blank_items, blank_items)
        return lax.fori_loop(0, clock_count, backward_clock_step, start_state)

    front_inputs = embedded[:half_count]
    back_inputs = embedded[half_count:]
    first_pass = forward_phase(front_inputs, back_inputs)
    second_pass = forward_phase(first_pass[5], first_pass[4])
    second_back = backward_phase(
        seed_grads[:half_count], seed_grads[half_count:], second_pass[3], second_pass[2]
    )
    first_back = backward_phase(second_back[5], second_back[4], first_pass[3], first_pass[2])
    inputs_first = jnp.concatenate([first_pass[2][0], second_pass[2][0]], axis=0)
    inputs_second = jnp.concatenate([first_pass[3][0], second_pass[3][0]], axis=0)
    grad_y_first = jnp.concatenate([first_back[3][0], second_back[3][0]], axis=0)
    grad_y_second = jnp.concatenate([first_back[2][0], second_back[2][0]], axis=0)
    grad_pre_first = jnp.concatenate([first_back[3][1], second_back[3][1]], axis=0)
    grad_pre_second = jnp.concatenate([first_back[2][1], second_back[2][1]], axis=0)
    act_first = jnp.concatenate([first_back[3][2], second_back[3][2]], axis=0)
    act_second = jnp.concatenate([first_back[2][2], second_back[2][2]], axis=0)
    term_in = jnp.stack(
        [
            jnp.einsum(
                "nrd,nrh->dh", inputs_first, grad_pre_first, preferred_element_type=jnp.float32
            ),
            jnp.einsum(
                "nrd,nrh->dh", inputs_second, grad_pre_second, preferred_element_type=jnp.float32
            ),
        ]
    )[None]
    term_out = jnp.stack(
        [
            jnp.einsum("nrh,nrd->hd", act_first, grad_y_first, preferred_element_type=jnp.float32),
            jnp.einsum(
                "nrh,nrd->hd", act_second, grad_y_second, preferred_element_type=jnp.float32
            ),
        ]
    )[None]
    grad_in, grad_out = (
        lax.psum_scatter(term_in, "dp", scatter_dimension=2, tiled=True),
        lax.psum_scatter(term_out, "dp", scatter_dimension=3, tiled=True),
    )
    return (grad_in, grad_out)


def solution(mesh):
    in_specs = (P(None, "dp"), P(), P(), P("pipe", None, None, None), P("pipe", None, None, None))
    out_specs = (P("pipe", None, "dp", None), P("pipe", None, None, "dp"))
    return jax.shard_map(local, mesh=mesh, in_specs=in_specs, out_specs=out_specs, check_vma=False)
```

profile of v0, /device:TPU:32, one launch (start us, length us, event | category | flops | bytes accessed | tf_op | source)
XLA Modules:
  0.0 1405.3 jit_solution(3516844705640671692)
XLA Ops:
  20.3 212.5 %while.112 = (s32[]{:T(128)}, bf16[32,3072]{1,0:T(8,128)(2,1)S(1)}, bf16[32,3072]{1,0:T(8,128)(2,1)S(1)}, bf16[2,32,3072]{2,1,0:T(8,128)(2,1)}, f32[2,32,256]{2,...) while((s32[]{:T(128)}, bf16[32,3072]{1,0:T(8,128)(2,1)S(1)}, ...), condition=%wide.region_2.3_spmd, body=%wide.region_1.2_spmd.sunk | while | flops 202604544 | bytes 26346988 | solution.py:121
  70.2 10.4 collective-permute-start
  96.5 9.0 collective-permute-start
  121.3 7.7 collective-permute-start
  192.0 7.7 collective-permute-start
  215.5 7.7 collective-permute-start
  235.7 206.3 %while.113 = (s32[]{:T(128)}, bf16[32,3072]{1,0:T(8,128)(2,1)S(1)}, bf16[32,3072]{1,0:T(8,128)(2,1)S(1)}, bf16[2,32,3072]{2,1,0:T(8,128)(2,1)}, f32[2,32,256]{2,...) while((s32[]{:T(128)}, bf16[32,3072]{1,0:T(8,128)(2,1)S(1)}, ...), condition=%wide.region_4.5_spmd, body=%wide.region_3.4_spmd.sunk | while | flops 202407936 | bytes 12191131 | solution.py:121
  402.7 7.7 collective-permute-start.2
  425.7 7.7 collective-permute-start.2
  446.1 217.8 %while.114 = (s32[]{:T(128)}, bf16[32,3072]{1,0:T(8,128)(2,1)S(1)}, bf16[32,3072]{1,0:T(8,128)(2,1)S(1)}, bf16[2,32,3072]{2,1,0:T(8,128)(2,1)}, bf16[2,32,256]{2...) while((s32[]{:T(128)}, bf16[32,3072]{1,0:T(8,128)(2,1)S(1)}, ...), condition=%wide.region_6.7_spmd, body=%wide.region_5.6_spmd.sunk | while | flops 202768384 | bytes 20055548 | solution.py:170
  476.9 7.7 collective-permute-start.4
  501.1 7.7 collective-permute-start.4
  525.3 7.7 collective-permute-start.4
  549.5 7.7 collective-permute-start.4
  573.7 7.7 collective-permute-start.4
  597.9 7.7 collective-permute-start.4
  622.1 7.7 collective-permute-start.4
  646.2 7.7 collective-permute-start.4
  666.2 189.6 %while.115 = (s32[]{:T(128)}, bf16[32,3072]{1,0:T(8,128)(2,1)S(1)}, bf16[32,3072]{1,0:T(8,128)(2,1)S(1)}, bf16[2,32,3072]{2,1,0:T(8,128)(2,1)}, bf16[2,32,256]{2...) while((s32[]{:T(128)}, bf16[32,3072]{1,0:T(8,128)(2,1)S(1)}, ...), condition=%wide.region_8.9_spmd, body=%wide.region_7.8_spmd.sunk | while | flops 202571776 | bytes 12453345 | solution.py:170
  670.5 7.7 collective-permute-start.6
  775.8 7.7 collective-permute-start.6
  861.3 10.2 copy.10
  880.6 336.3 %all-reduce.3.cloned.1.call-done = f32[1,2,256,3072]{2,1,0,3:T(2,128)} async-done(((f32[1,2,256,3072]{2,1,0,3:T(2,128)}), f32[1,2,256,3072]{2,1,0,3:T(2,128)}) %all-reduce.3.cloned.1.call-update) | async-done | bytes 6291472
  1218.6 179.9 %reduce-scatter.2.cloned.1.call-done = f32[1,2,96,256]{3,2,1,0:T(8,128)} async-done(((f32[1,2,3072,256]{3,2,1,0:T(8,128)}), f32[1,2,96,256]{3,2,1,0:T(8,128)}) %reduce-scatter.2.cloned.1.call-update) | async-done | bytes 196624 | tf_op jit(solution)/shard_map/reduce_scatter | solution.py:207
  (661 shorter events, 726.7 us)
Async XLA Ops:
  7.2 1209.8 %all-reduce.3.cloned.1.call-start = ((), (), s32[]{:S(2)}) async-start(), calls=%async_computation.2 | async-start | bytes 12582912
  70.2 17.9 %collective-permute-start = (bf16[32,3072]{1,0:T(8,128)(2,1)S(1)}, bf16[32,3072]{1,0:T(8,128)(2,1)S(1)}, u32[]{:S(2)}, u32[]{:S(2)}) collective-permute-start(bf16[32,3072]{1,0:T(8,128)(2,1)S(1)} %get-tuple-element.2156), channel_id=1, source_target_pairs={{0,32},{32,64},{64,96},{96,128},{128,160},{160,192},{192,224},{1,3... | collective-permute-start | bytes 589832 | tf_op jit(solution)/shard_map/while/body/eval_jaxpr/ppermute | solution.py:12
  96.5 16.5 %collective-permute-start = (bf16[32,3072]{1,0:T(8,128)(2,1)S(1)}, bf16[32,3072]{1,0:T(8,128)(2,1)S(1)}, u32[]{:S(2)}, u32[]{:S(2)}) collective-permute-start(bf16[32,3072]{1,0:T(8,128)(2,1)S(1)} %get-tuple-element.2156), channel_id=1, source_target_pairs={{0,32},{32,64},{64,96},{96,128},{128,160},{160,192},{192,224},{1,3... | collective-permute-start | bytes 589832 | tf_op jit(solution)/shard_map/while/body/eval_jaxpr/ppermute | solution.py:12
  121.3 15.3 %collective-permute-start = (bf16[32,3072]{1,0:T(8,128)(2,1)S(1)}, bf16[32,3072]{1,0:T(8,128)(2,1)S(1)}, u32[]{:S(2)}, u32[]{:S(2)}) collective-permute-start(bf16[32,3072]{1,0:T(8,128)(2,1)S(1)} %get-tuple-element.2156), channel_id=1, source_target_pairs={{0,32},{32,64},{64,96},{96,128},{128,160},{160,192},{192,224},{1,3... | collective-permute-start | bytes 589832 | tf_op jit(solution)/shard_map/while/body/eval_jaxpr/ppermute | solution.py:12
  215.5 15.3 %collective-permute-start = (bf16[32,3072]{1,0:T(8,128)(2,1)S(1)}, bf16[32,3072]{1,0:T(8,128)(2,1)S(1)}, u32[]{:S(2)}, u32[]{:S(2)}) collective-permute-start(bf16[32,3072]{1,0:T(8,128)(2,1)S(1)} %get-tuple-element.2156), channel_id=1, source_target_pairs={{0,32},{32,64},{64,96},{96,128},{128,160},{160,192},{192,224},{1,3... | collective-permute-start | bytes 589832 | tf_op jit(solution)/shard_map/while/body/eval_jaxpr/ppermute | solution.py:12
  452.7 17.1 %collective-permute-start.4 = (bf16[32,3072]{1,0:T(8,128)(2,1)S(1)}, bf16[32,3072]{1,0:T(8,128)(2,1)S(1)}, u32[]{:S(2)}, u32[]{:S(2)}) collective-permute-start(bf16[32,3072]{1,0:T(8,128)(2,1)S(1)} %get-tuple-element.2218), channel_id=1, source_target_pairs={{0,32},{32,64},{64,96},{96,128},{128,160},{160,192},{192,224},{1,3... | collective-permute-start | bytes 589832 | tf_op jit(solution)/shard_map/while/body/eval_jaxpr/ppermute | solution.py:12
  476.9 17.1 %collective-permute-start.4 = (bf16[32,3072]{1,0:T(8,128)(2,1)S(1)}, bf16[32,3072]{1,0:T(8,128)(2,1)S(1)}, u32[]{:S(2)}, u32[]{:S(2)}) collective-permute-start(bf16[32,3072]{1,0:T(8,128)(2,1)S(1)} %get-tuple-element.2218), channel_id=1, source_target_pairs={{0,32},{32,64},{64,96},{96,128},{128,160},{160,192},{192,224},{1,3... | collective-permute-start | bytes 589832 | tf_op jit(solution)/shard_map/while/body/eval_jaxpr/ppermute | solution.py:12
  501.1 17.1 %collective-permute-start.4 = (bf16[32,3072]{1,0:T(8,128)(2,1)S(1)}, bf16[32,3072]{1,0:T(8,128)(2,1)S(1)}, u32[]{:S(2)}, u32[]{:S(2)}) collective-permute-start(bf16[32,3072]{1,0:T(8,128)(2,1)S(1)} %get-tuple-element.2218), channel_id=1, source_target_pairs={{0,32},{32,64},{64,96},{96,128},{128,160},{160,192},{192,224},{1,3... | collective-permute-start | bytes 589832 | tf_op jit(solution)/shard_map/while/body/eval_jaxpr/ppermute | solution.py:12
  525.3 17.1 %collective-permute-start.4 = (bf16[32,3072]{1,0:T(8,128)(2,1)S(1)}, bf16[32,3072]{1,0:T(8,128)(2,1)S(1)}, u32[]{:S(2)}, u32[]{:S(2)}) collective-permute-start(bf16[32,3072]{1,0:T(8,128)(2,1)S(1)} %get-tuple-element.2218), channel_id=1, source_target_pairs={{0,32},{32,64},{64,96},{96,128},{128,160},{160,192},{192,224},{1,3... | collective-permute-start | bytes 589832 | tf_op jit(solution)/shard_map/while/body/eval_jaxpr/ppermute | solution.py:12
  549.5 17.1 %collective-permute-start.4 = (bf16[32,3072]{1,0:T(8,128)(2,1)S(1)}, bf16[32,3072]{1,0:T(8,128)(2,1)S(1)}, u32[]{:S(2)}, u32[]{:S(2)}) collective-permute-start(bf16[32,3072]{1,0:T(8,128)(2,1)S(1)} %get-tuple-element.2218), channel_id=1, source_target_pairs={{0,32},{32,64},{64,96},{96,128},{128,160},{160,192},{192,224},{1,3... | collective-permute-start | bytes 589832 | tf_op jit(solution)/shard_map/while/body/eval_jaxpr/ppermute | solution.py:12
  573.7 17.1 %collective-permute-start.4 = (bf16[32,3072]{1,0:T(8,128)(2,1)S(1)}, bf16[32,3072]{1,0:T(8,128)(2,1)S(1)}, u32[]{:S(2)}, u32[]{:S(2)}) collective-permute-start(bf16[32,3072]{1,0:T(8,128)(2,1)S(1)} %get-tuple-element.2218), channel_id=1, source_target_pairs={{0,32},{32,64},{64,96},{96,128},{128,160},{160,192},{192,224},{1,3... | collective-permute-start | bytes 589832 | tf_op jit(solution)/shard_map/while/body/eval_jaxpr/ppermute | solution.py:12
  597.9 17.1 %collective-permute-start.4 = (bf16[32,3072]{1,0:T(8,128)(2,1)S(1)}, bf16[32,3072]{1,0:T(8,128)(2,1)S(1)}, u32[]{:S(2)}, u32[]{:S(2)}) collective-permute-start(bf16[32,3072]{1,0:T(8,128)(2,1)S(1)} %get-tuple-element.2218), channel_id=1, source_target_pairs={{0,32},{32,64},{64,96},{96,128},{128,160},{160,192},{192,224},{1,3... | collective-permute-start | bytes 589832 | tf_op jit(solution)/shard_map/while/body/eval_jaxpr/ppermute | solution.py:12
  622.1 17.1 %collective-permute-start.4 = (bf16[32,3072]{1,0:T(8,128)(2,1)S(1)}, bf16[32,3072]{1,0:T(8,128)(2,1)S(1)}, u32[]{:S(2)}, u32[]{:S(2)}) collective-permute-start(bf16[32,3072]{1,0:T(8,128)(2,1)S(1)} %get-tuple-element.2218), channel_id=1, source_target_pairs={{0,32},{32,64},{64,96},{96,128},{128,160},{160,192},{192,224},{1,3... | collective-permute-start | bytes 589832 | tf_op jit(solution)/shard_map/while/body/eval_jaxpr/ppermute | solution.py:12
  646.2 17.1 %collective-permute-start.4 = (bf16[32,3072]{1,0:T(8,128)(2,1)S(1)}, bf16[32,3072]{1,0:T(8,128)(2,1)S(1)}, u32[]{:S(2)}, u32[]{:S(2)}) collective-permute-start(bf16[32,3072]{1,0:T(8,128)(2,1)S(1)} %get-tuple-element.2218), channel_id=1, source_target_pairs={{0,32},{32,64},{64,96},{96,128},{128,160},{160,192},{192,224},{1,3... | collective-permute-start | bytes 589832 | tf_op jit(solution)/shard_map/while/body/eval_jaxpr/ppermute | solution.py:12
  670.5 16.2 %collective-permute-start.6 = (bf16[32,3072]{1,0:T(8,128)(2,1)S(1)}, bf16[32,3072]{1,0:T(8,128)(2,1)S(1)}, u32[]{:S(2)}, u32[]{:S(2)}) collective-permute-start(bf16[32,3072]{1,0:T(8,128)(2,1)S(1)} %fusion.167), channel_id=1, source_target_pairs={{0,32},{32,64},{64,96},{96,128},{128,160},{160,192},{192,224},{1,3... | collective-permute-start | bytes 589832 | tf_op jit(solution)/shard_map/while/body/eval_jaxpr/ppermute | solution.py:12
  691.5 16.2 %collective-permute-start.6 = (bf16[32,3072]{1,0:T(8,128)(2,1)S(1)}, bf16[32,3072]{1,0:T(8,128)(2,1)S(1)}, u32[]{:S(2)}, u32[]{:S(2)}) collective-permute-start(bf16[32,3072]{1,0:T(8,128)(2,1)S(1)} %fusion.167), channel_id=1, source_target_pairs={{0,32},{32,64},{64,96},{96,128},{128,160},{160,192},{192,224},{1,3... | collective-permute-start | bytes 589832 | tf_op jit(solution)/shard_map/while/body/eval_jaxpr/ppermute | solution.py:12
  712.6 16.2 %collective-permute-start.6 = (bf16[32,3072]{1,0:T(8,128)(2,1)S(1)}, bf16[32,3072]{1,0:T(8,128)(2,1)S(1)}, u32[]{:S(2)}, u32[]{:S(2)}) collective-permute-start(bf16[32,3072]{1,0:T(8,128)(2,1)S(1)} %fusion.167), channel_id=1, source_target_pairs={{0,32},{32,64},{64,96},{96,128},{128,160},{160,192},{192,224},{1,3... | collective-permute-start | bytes 589832 | tf_op jit(solution)/shard_map/while/body/eval_jaxpr/ppermute | solution.py:12
  733.7 16.2 %collective-permute-start.6 = (bf16[32,3072]{1,0:T(8,128)(2,1)S(1)}, bf16[32,3072]{1,0:T(8,128)(2,1)S(1)}, u32[]{:S(2)}, u32[]{:S(2)}) collective-permute-start(bf16[32,3072]{1,0:T(8,128)(2,1)S(1)} %fusion.167), channel_id=1, source_target_pairs={{0,32},{32,64},{64,96},{96,128},{128,160},{160,192},{192,224},{1,3... | collective-permute-start | bytes 589832 | tf_op jit(solution)/shard_map/while/body/eval_jaxpr/ppermute | solution.py:12
  754.7 16.2 %collective-permute-start.6 = (bf16[32,3072]{1,0:T(8,128)(2,1)S(1)}, bf16[32,3072]{1,0:T(8,128)(2,1)S(1)}, u32[]{:S(2)}, u32[]{:S(2)}) collective-permute-start(bf16[32,3072]{1,0:T(8,128)(2,1)S(1)} %fusion.167), channel_id=1, source_target_pairs={{0,32},{32,64},{64,96},{96,128},{128,160},{160,192},{192,224},{1,3... | collective-permute-start | bytes 589832 | tf_op jit(solution)/shard_map/while/body/eval_jaxpr/ppermute | solution.py:12
  775.8 16.2 %collective-permute-start.6 = (bf16[32,3072]{1,0:T(8,128)(2,1)S(1)}, bf16[32,3072]{1,0:T(8,128)(2,1)S(1)}, u32[]{:S(2)}, u32[]{:S(2)}) collective-permute-start(bf16[32,3072]{1,0:T(8,128)(2,1)S(1)} %fusion.167), channel_id=1, source_target_pairs={{0,32},{32,64},{64,96},{96,128},{128,160},{160,192},{192,224},{1,3... | collective-permute-start | bytes 589832 | tf_op jit(solution)/shard_map/while/body/eval_jaxpr/ppermute | solution.py:12
  796.9 16.2 %collective-permute-start.6 = (bf16[32,3072]{1,0:T(8,128)(2,1)S(1)}, bf16[32,3072]{1,0:T(8,128)(2,1)S(1)}, u32[]{:S(2)}, u32[]{:S(2)}) collective-permute-start(bf16[32,3072]{1,0:T(8,128)(2,1)S(1)} %fusion.167), channel_id=1, source_target_pairs={{0,32},{32,64},{64,96},{96,128},{128,160},{160,192},{192,224},{1,3... | collective-permute-start | bytes 589832 | tf_op jit(solution)/shard_map/while/body/eval_jaxpr/ppermute | solution.py:12
  818.0 16.2 %collective-permute-start.6 = (bf16[32,3072]{1,0:T(8,128)(2,1)S(1)}, bf16[32,3072]{1,0:T(8,128)(2,1)S(1)}, u32[]{:S(2)}, u32[]{:S(2)}) collective-permute-start(bf16[32,3072]{1,0:T(8,128)(2,1)S(1)} %fusion.167), channel_id=1, source_target_pairs={{0,32},{32,64},{64,96},{96,128},{128,160},{160,192},{192,224},{1,3... | collective-permute-start | bytes 589832 | tf_op jit(solution)/shard_map/while/body/eval_jaxpr/ppermute | solution.py:12
  839.0 16.2 %collective-permute-start.6 = (bf16[32,3072]{1,0:T(8,128)(2,1)S(1)}, bf16[32,3072]{1,0:T(8,128)(2,1)S(1)}, u32[]{:S(2)}, u32[]{:S(2)}) collective-permute-start(bf16[32,3072]{1,0:T(8,128)(2,1)S(1)} %fusion.167), channel_id=1, source_target_pairs={{0,32},{32,64},{64,96},{96,128},{128,160},{160,192},{192,224},{1,3... | collective-permute-start | bytes 589832 | tf_op jit(solution)/shard_map/while/body/eval_jaxpr/ppermute | solution.py:12
  871.5 526.9 %reduce-scatter.2.cloned.1.call-start = ((), (), s32[]{:S(2)}) async-start(), calls=%async_computation.1 | async-start | bytes 6488064 | tf_op jit(solution)/shard_map/reduce_scatter | solution.py:207
  (99 other events, 1205.6 us)
Sparse Core Ops, SparseCore 0:
  871.7 345.2 all-reduce.2
  1220.1 178.3 reduce-scatter.1
where the time goes:
time: 1420 us; the launch traced here: 1410 us
  waiting for transfers between devices  566 us (40%)
  starting transfers between devices  321 us (23%)
  matrix products  228 us (16%)
  local copies, waits for them, and re-layouts  149 us (10%)
  other arithmetic  124 us (9%)
  between operations  14.9 us (1%)
    unnamed x3, waiting for transfers between devices  336 us
    ppermute x72, starting transfers between devices, from_behind(): return lax.ppermute(x, axis, pairs)  321 us
    reduce_scatter x1, waiting for transfers between devices, local(): lax.psum_scatter(term_in, 'dp', scatter_dimension=2, tiled=True)  180 us
    dynamic_update_slice x90, other arithmetic, place_item(): lax.dynamic_update_index_in_dim(buffer, jnp.where(is_live, fresh_value, p...  117 us
    dynamic_slice x144, local copies, waits for them, and re-layouts, place_item(): previous = lax.dynamic_index_in_dim(buffer, slot_index, 0, keepdims=False)  114 us
    dot_general x36, matrix products, retreat(): jnp.einsum('rd,hd->rh', grad_y, w_second, preferred_element_type=jnp.floa...  82.4 us
    dot_general x36, matrix products, advance(): pre_act = jnp.dot(inputs, w_first, preferred_element_type=jnp.float32)  67.7 us
    ppermute x72, waiting for transfers between devices, from_behind(): return lax.ppermute(x, axis, pairs)  50.1 us
  transfers between devices with their start and end apart: 74, of which 38 were waited for; matrix products, arithmetic and copies ran while one was open for 18% of the time, Pallas kernels for 0%

commit v1 on v0

v1 whole, which is shorter than its diff:
```python
import functools
import math

import jax
import jax.numpy as jnp
from jax import lax
from jax.experimental import pallas as pl
from jax.experimental.pallas import tpu as pltpu
from jax.sharding import PartitionSpec as P

MESH = pl.DeviceIdType.MESH
F32 = jnp.float32
BF16 = jnp.bfloat16


def mm(a, b):
    return jnp.dot(a, b, preferred_element_type=F32)


def mm_t(a, b):
    return lax.dot_general(a, b, (((1,), (1,)), ((), ())), preferred_element_type=F32)


def t_mm(a, b):
    return lax.dot_general(a, b, (((0,), (0,)), ((), ())), preferred_element_type=F32)


def fold(wide):
    half = wide.shape[1] // 2
    return jnp.concatenate([wide[:, :half], wide[:, half:]], axis=0)


def twice(rows):
    return jnp.concatenate([rows, rows], axis=0).astype(BF16)


def kernel(
    n_pipe,
    n_dp,
    scale,
    ids_ref,
    cand_ref,
    win_ref,
    wout_ref,
    gin_ref,
    gout_ref,
    w_in,
    w_out,
    got,
    give,
    pres,
    ids_all,
    sbuf,
    rbuf,
    w_sem,
    give_sem,
    got_sem,
    ids_send,
    ids_recv,
    x_send,
    x_recv,
):
    p = lax.axis_index("pipe")
    d = lax.axis_index("dp")
    half_dp = n_dp // 2
    path = d // half_dp
    block = d % half_dp
    c1 = path
    c2 = 1 - path
    last = n_pipe - 1
    q = p + path * (last - 2 * p)
    up = p + 1 - 2 * path
    down = p - 1 + 2 * path
    half = w_in.shape[1] // 2
    share = 2 * half // n_dp

    def load(c):
        return (
            pltpu.make_async_copy(win_ref.at[0, c], w_in.at[c], w_sem.at[c, 0]),
            pltpu.make_async_copy(wout_ref.at[0, c], w_out.at[c], w_sem.at[c, 1]),
        )

    for c in (c1, c2):
        for copy in load(c):
            copy.start()

    barrier = pltpu.get_barrier_semaphore()
    for step in (1, n_pipe - 1):
        pl.semaphore_signal(
            barrier, inc=1, device_id={"pipe": lax.rem(p + step, n_pipe)}, device_id_type=MESH
        )

    def greet(k, carry):
        pl.semaphore_signal(
            barrier, inc=1, device_id={"dp": lax.rem(d + k, n_dp)}, device_id_type=MESH
        )
        return carry

    lax.fori_loop(1, n_dp, greet, 0)
    pl.semaphore_wait(barrier, n_dp + 1)

    def hop(slot, to):
        return pltpu.make_async_remote_copy(
            src_ref=give.at[slot],
            dst_ref=got.at[slot],
            send_sem=give_sem.at[slot],
            recv_sem=got_sem.at[slot],
            device_id={"pipe": to},
            device_id_type=MESH,
        )

    def spread_ids():
        ids_all[d] = ids_ref[...]

        def send(k, carry):
            pltpu.make_async_remote_copy(
                src_ref=ids_ref,
                dst_ref=ids_all.at[d],
                send_sem=ids_send,
                recv_sem=ids_recv,
                device_id={"dp": lax.rem(d + k, n_dp)},
                device_id_type=MESH,
            ).start()
            return carry

        lax.fori_loop(1, n_dp, send, 0)

    def spread(c, kind, small, big):
        hidden = small.shape[1] // 2
        top = jnp.concatenate([small[:, :hidden], small[:, hidden:]], axis=0).astype(BF16)
        wide = jnp.concatenate([big, big[:, :128]], axis=1)
        for j in range(half_dp):
            sbuf[c, kind, j, 0:16, :] = top
            sbuf[c, kind, j, 16:32, :] = wide[:, share * j : share * j + 128].astype(BF16)
        rbuf[c, kind, d] = sbuf[c, kind, block]

        def send(k, carry):
            peer = lax.rem(d + k, n_dp)
            pltpu.make_async_remote_copy(
                src_ref=sbuf.at[c, kind, lax.rem(peer, half_dp)],
                dst_ref=rbuf.at[c, kind, d],
                send_sem=x_send.at[c, kind],
                recv_sem=x_recv.at[c, kind],
                device_id={"dp": peer},
                device_id_type=MESH,
            ).start()
            return carry

        lax.fori_loop(1, n_dp, send, 0)

    def many(ref, sem):
        return pltpu.make_async_copy(ref, ref, sem)

    def forward(c, slot):
        x2 = got[slot]
        pre = mm(x2, w_in[c, :half, :])[:8] + mm(x2, w_in[c, half:, :])[8:]
        act = pre / (1.0 + jnp.exp(-pre))
        pres[c] = pre
        branch = mm(twice(act), w_out[c])[:8]
        y2 = (x2.astype(F32) + fold(branch)).astype(BF16)
        give[slot] = y2
        return x2, act

    def backward(c, slot, want):
        g2 = got[slot]
        grad_act = mm_t(g2, w_out[c, :, :half])[:8] + mm_t(g2, w_out[c, :, half:])[8:]
        pre = pres[c]
        logistic = 1.0 / (1.0 + jnp.exp(-pre))
        grad_pre = grad_act * (logistic * (1.0 + pre * (1.0 - logistic)))

        @pl.when(want)
        def _():
            term = mm_t(twice(grad_pre), w_in[c])[:8]
            give[slot] = (g2.astype(F32) + fold(term)).astype(BF16)

        return g2, grad_pre

    def finish(c):
        for kind in (0, 1):
            many(rbuf.at[c, kind, pl.ds(0, n_dp - 1)], x_recv.at[c, kind]).wait()

        def unpack(kind):
            rows = rbuf[c, kind].astype(F32)
            flat = lambda part: part.reshape(n_dp * 8, 128)
            small = jnp.concatenate([flat(rows[:, 0:8]), flat(rows[:, 8:16])], axis=1)
            big = jnp.where(path == 0, flat(rows[:, 16:24]), flat(rows[:, 24:32]))
            return small.astype(BF16), big.astype(BF16)

        act, x = unpack(0)
        grad_pre, grad_y = unpack(1)
        gin_ref[0, c] = t_mm(x, grad_pre)[:share]
        gout_ref[0, c] = t_mm(act, grad_y)[:, :share]

    @pl.when(q == last)
    def _():
        spread_ids()

    @pl.when(q == 0)
    def _():
        start = pl.multiple_of(16 * (block // 2), 16)
        rows = cand_ref[pl.ds(start, 16), :].astype(F32)
        mine = jnp.where(block % 2 == 0, rows[:8], rows[8:])
        got[0] = fold(mine).astype(BF16)

    @pl.when(q > 0)
    def _():
        hop(0, down).wait_recv()

    for copy in load(c1):
        copy.wait()
    x2, act = forward(c1, 0)

    @pl.when(q < last)
    def _():
        hop(0, up).start()

    @pl.when(q == last)
    def _():
        got[1] = give[0]

    @pl.when(q == 0)
    def _():
        spread_ids()

    spread(c1, 0, act, x2.astype(F32))

    @pl.when((q == 0) | (q == last))
    def _():
        many(ids_all.at[pl.ds(0, n_dp - 1)], ids_recv).wait()

    @pl.when(q == 0)
    def _():
        own = lax.broadcasted_iota(jnp.int32, (16, 128), 0) + 8 * block
        every = lax.broadcasted_iota(jnp.int32, (128, 128), 0)

        def count(group, total):
            left, right = [], []
            for k in range(8):
                tile = ids_all[group * 8 + k]
                events = jnp.where(path == 0, tile[0:1, :], tile[1:2, :])
                left.append(jnp.where(own == events, 1.0, 0.0).astype(BF16))
                right.append(jnp.where(every == tile[2:3, :], 1.0, 0.0).astype(BF16))
            return total + mm_t(jnp.concatenate(left, axis=1), jnp.concatenate(right, axis=1))

        counts = lax.fori_loop(0, n_dp // 8, count, jnp.zeros((16, 128), F32))[:8]
        sixteens = jnp.floor(counts * 0.0625)
        parts = jnp.concatenate([sixteens, counts - 16.0 * sixteens], axis=0).astype(BF16)
        sums = mm(parts, cand_ref[...])
        got[2] = fold((16.0 * sums[:8] + sums[8:]) * scale).astype(BF16)

    @pl.when(q < last)
    def _():
        hop(1, up).wait_recv()

    for copy in load(c2):
        copy.wait()
    x2, act = forward(c2, 1)

    @pl.when(q > 0)
    def _():
        hop(1, down).start()

    spread(c2, 0, act, x2.astype(F32))

    @pl.when(q > 0)
    def _():
        hop(2, down).wait_recv()

    g2, grad_pre = backward(c2, 2, q >= 0)

    @pl.when(q < last)
    def _():
        hop(2, up).start()

    @pl.when(q == last)
    def _():
        got[3] = give[2]

    spread(c2, 1, grad_pre, g2.astype(F32))

    @pl.when(q <= 2)
    def _():
        finish(c2)

    @pl.when(q < last)
    def _():
        hop(3, up).wait_recv()

    g2, grad_pre = backward(c1, 3, q > 0)

    @pl.when(q > 0)
    def _():
        hop(3, down).start()

    spread(c1, 1, grad_pre, g2.astype(F32))
    finish(c1)

    @pl.when(q > 2)
    def _():
        finish(c2)

    @pl.when(q < last)
    def _():
        hop(0, up).wait_send()
        hop(2, up).wait_send()

    @pl.when(q > 0)
    def _():
        hop(1, down).wait_send()
        hop(3, down).wait_send()

    @pl.when((q == 0) | (q == last))
    def _():
        many(ids_all.at[pl.ds(0, n_dp - 1)], ids_send).wait()

    for c in (0, 1):
        for kind in (0, 1):
            many(rbuf.at[c, kind, pl.ds(0, n_dp - 1)], x_send.at[c, kind]).wait()


def local(n_pipe, n_dp, item_ids, plan_order, candidates, adapters_in, adapters_out):
    batches, width = item_ids.shape
    events = width - 1
    _, _, features, hidden = adapters_in.shape
    share = features // n_dp
    scale = 1.0 / math.sqrt(batches * n_dp * events)
    event = item_ids[:, :events].reshape(1, batches * events)
    target = item_ids[:, 1:].reshape(1, batches * events)
    front = jnp.repeat(plan_order < batches // 2, events).reshape(1, batches * events)
    ids = jnp.concatenate(
        [
            jnp.where(front, event, -1),
            jnp.where(front, -1, event),
            target,
            jnp.zeros((5, batches * events), jnp.int32),
        ],
        axis=0,
    )
    vmem = pl.BlockSpec(memory_space=pltpu.VMEM)
    anywhere = pl.BlockSpec(memory_space=pl.ANY)
    return pl.pallas_call(
        functools.partial(kernel, n_pipe, n_dp, scale),
        out_shape=(
            jax.ShapeDtypeStruct((1, 2, share, hidden), F32),
            jax.ShapeDtypeStruct((1, 2, hidden, share), F32),
        ),
        in_specs=[vmem, vmem, anywhere, anywhere],
        out_specs=(vmem, vmem),
        scratch_shapes=[
            pltpu.VMEM((2, features, hidden), BF16),
            pltpu.VMEM((2, hidden, features), BF16),
            pltpu.VMEM((4, 16, features // 2), BF16),
            pltpu.VMEM((4, 16, features // 2), BF16),
            pltpu.VMEM((2, 8, hidden), F32),
            pltpu.VMEM((n_dp, 8, 128), jnp.int32),
            pltpu.VMEM((2, 2, n_dp // 2, 32, 128), BF16),
            pltpu.VMEM((2, 2, n_dp, 32, 128), BF16),
            pltpu.SemaphoreType.DMA((2, 2)),
            pltpu.SemaphoreType.DMA((4,)),
            pltpu.SemaphoreType.DMA((4,)),
            pltpu.SemaphoreType.DMA,
            pltpu.SemaphoreType.DMA,
            pltpu.SemaphoreType.DMA((2, 2)),
            pltpu.SemaphoreType.DMA((2, 2)),
        ],
        compiler_params=pltpu.CompilerParams(
            collective_id=0, has_side_effects=True, vmem_limit_bytes=40 * 1024 * 1024
        ),
    )(ids, candidates, adapters_in, adapters_out)


def solution(mesh):
    in_specs = (P(None, "dp"), P(), P(), P("pipe", None, None, None), P("pipe", None, None, None))
    out_specs = (P("pipe", None, "dp", None), P("pipe", None, None, "dp"))
    return jax.shard_map(
        functools.partial(local, mesh.shape["pipe"], mesh.shape["dp"]),
        mesh=mesh,
        in_specs=in_specs,
        out_specs=out_specs,
        check_vma=False,
    )
```

time: 1420 us -> 108 us (0.08); the launches traced: 1410 us -> 107 us
  waiting for transfers between devices: 566 us -> 0 us
  starting transfers between devices: 321 us -> 0 us
  matrix products: 228 us -> 0 us
  local copies, waits for them, and re-layouts: 149 us -> 6.72 us
  other arithmetic: 124 us -> 1.56 us
  Pallas kernels: 0 us -> 98.6 us
  between operations: 14.9 us -> 0.65 us
    unnamed x3 -> x0, waiting for transfers between devices: 336 us -> none
    ppermute x72 -> x0, starting transfers between devices: 321 us -> none  [from_behind(): return lax.ppermute(x, axis, pairs)]
    dot_general x150 -> x0, matrix products: 228 us -> none  [the longest x36 82.4 us: retreat(): jnp.einsum('rd,hd->rh', grad_y, w_second, preferred_element_type=jnp.floa...]
    reduce_scatter x1 -> x0, waiting for transfers between devices: 180 us -> none  [local(): lax.psum_scatter(term_in, 'dp', scatter_dimension=2, tiled=True)]
    dynamic_update_slice x90 -> x0, other arithmetic: 117 us -> none  [place_item(): lax.dynamic_update_index_in_dim(buffer, jnp.where(is_live, fresh_value, p...]
    dynamic_slice x144 -> x0, local copies, waits for them, and re-layouts: 114 us -> none  [place_item(): previous = lax.dynamic_index_in_dim(buffer, slot_index, 0, keepdims=False)]
    pallas_call x0 -> x1, Pallas kernels: none -> 98.6 us  [local(): pl.pallas_call(functools.partial(kernel, n_pipe, n_dp, scale), out_shape=...]
    ppermute x72 -> x0, waiting for transfers between devices: 50.1 us -> none  [from_behind(): return lax.ppermute(x, axis, pairs)]
  transfers between devices with their start and end apart: 74 -> 0, of which waited for: 38 -> 0; matrix products, arithmetic and copies ran while one was open for 18% -> 0% of each run, Pallas kernels for 0% -> 0%
where the time goes in v1:
time: 108 us; the launch traced here: 107 us
  Pallas kernels  98.6 us (91%)
  local copies, waits for them, and re-layouts  6.72 us (6%)
  other arithmetic  1.56 us (1%)
    pallas_call x1, Pallas kernels, local(): pl.pallas_call(functools.partial(kernel, n_pipe, n_dp, scale), out_shape=...  98.6 us
    unnamed x7, local copies, waits for them, and re-layouts  5.59 us

profile of v1, /device:TPU:32, one launch (start us, length us, event | category | flops | bytes accessed | tf_op | source)
XLA Modules:
  0.0 107.5 jit_solution(14761286413087958317)
XLA Ops:
  0.6 0.7 broadcast_compare_fusion
  1.3 0.1 pad.3.clone
  1.4 0.8 slice_select_fusion.1
  2.2 0.1 select_n.31
  2.3 0.1 select_n.33
  2.4 0.1 reshape.52
  2.4 0.1 add_add_fusion.ids_ref
  2.5 0.0 copy-start
  2.5 1.9 %copy-done = bf16[1,2,3072,256]{3,2,1,0:T(8,128)(2,1)S(1)} copy-done((bf16[1,2,3072,256]{3,2,1,0:T(8,128)(2,1)S(1)}, bf16[1,2,3072,256]{3,2,1,0:T(8,128)(2,1)}, u32[]{:S(2)}) %copy-start) | copy-done | bytes 3145752
  4.4 0.0 copy-start.1
  4.4 1.9 %copy-done.1 = bf16[1,2,256,3072]{3,2,1,0:T(8,128)(2,1)S(1)} copy-done((bf16[1,2,256,3072]{3,2,1,0:T(8,128)(2,1)S(1)}, bf16[1,2,256,3072]{3,2,1,0:T(8,128)(2,1)}, u32[]{:S(2)}) %copy-start.1) | copy-done | bytes 3145752
  6.3 0.0 copy-start.2
  6.3 1.1 %copy-done.2 = bf16[128,3072]{1,0:T(8,128)(2,1)S(1)} copy-done((bf16[128,3072]{1,0:T(8,128)(2,1)S(1)}, bf16[128,3072]{1,0:T(8,128)(2,1)}, u32[]{:S(2)}) %copy-start.2) | copy-done | bytes 786456
  7.4 98.6 %shard_map.68 = (f32[1,2,96,256]{3,2,1,0:T(8,128)S(1)}, f32[1,2,256,96]{3,2,1,0:T(8,128)S(1)}) custom-call(s32[8,128]{1,0:T(8,128)S(1)} %add_add_fusion.ids_ref, bf16[128,3072]{1,0:T(8,128)(2,1)S(1)} %copy-done.2, bf16[1,2,3072,256]{3,2,1,0:T(8,128)(2,1)S(1)} %copy-done, bf16[1,2,256,3072]{3,2,1,0:T(8,128)(2,1)S(1)} %copy-done.1), custom_call_target="tpu_custom_call" | custom-call | tf_op jit(solution)/shard_map/pallas_call | solution.py:341
  106.0 0.8 copy.7
  106.8 0.7 copy.9
  (1 shorter events, 0.0 us)
Async XLA Ops:
  2.5 1.9 %copy-start = (bf16[1,2,3072,256]{3,2,1,0:T(8,128)(2,1)S(1)}, bf16[1,2,3072,256]{3,2,1,0:T(8,128)(2,1)}, u32[]{:S(2)}) copy-start(bf16[1,2,3072,256]{3,2,1,0:T(8,128)(2,1)} %win_ref.1) | copy-start | bytes 9437188
  4.4 1.9 %copy-start.1 = (bf16[1,2,256,3072]{3,2,1,0:T(8,128)(2,1)S(1)}, bf16[1,2,256,3072]{3,2,1,0:T(8,128)(2,1)}, u32[]{:S(2)}) copy-start(bf16[1,2,256,3072]{3,2,1,0:T(8,128)(2,1)} %wout_ref.1) | copy-start | bytes 9437188
  6.3 1.1 %copy-start.2 = (bf16[128,3072]{1,0:T(8,128)(2,1)S(1)}, bf16[128,3072]{1,0:T(8,128)(2,1)}, u32[]{:S(2)}) copy-start(bf16[128,3072]{1,0:T(8,128)(2,1)} %cand_ref.1) | copy-start | bytes 2359300

commit v2 on v1

v2 whole, which is shorter than its diff:
```python
import functools
import math

import jax
import jax.numpy as jnp
from jax import lax
from jax.experimental import pallas as pl
from jax.experimental.pallas import tpu as pltpu
from jax.sharding import PartitionSpec as P

MESH = pl.DeviceIdType.MESH
F32 = jnp.float32
BF16 = jnp.bfloat16
PIECES = 3


def mm(a, b):
    return jnp.dot(a, b, preferred_element_type=F32)


def mm_t(a, b):
    return lax.dot_general(a, b, (((1,), (1,)), ((), ())), preferred_element_type=F32)


def t_mm(a, b):
    return lax.dot_general(a, b, (((0,), (0,)), ((), ())), preferred_element_type=F32)


def fold(wide):
    half = wide.shape[1] // 2
    return jnp.concatenate([wide[:, :half], wide[:, half:]], axis=0)


def twice(rows):
    return jnp.concatenate([rows, rows], axis=0).astype(BF16)


def kernel(
    n_pipe,
    n_dp,
    scale,
    ids_hbm,
    cand_hbm,
    win_ref,
    wout_ref,
    gin_ref,
    gout_ref,
    w_in,
    w_out,
    t_in,
    t_out,
    m_fwd,
    m_bwd,
    ids_ref,
    cand_ref,
    first_rows,
    ids_own,
    ids_all,
    got,
    mid,
    give,
    small,
    slopes,
    mail_big,
    mail_small,
    sbuf,
    rbuf,
    x_turned,
    act_rows,
    w_sem,
    cand_sem,
    share_send,
    share_recv,
    give_sem,
    got_sem,
    mail_send,
    mail_recv,
    back_send,
    back_recv,
    ids_send,
    ids_recv,
    x_send,
    x_recv,
):
    p = lax.axis_index("pipe")
    d = lax.axis_index("dp")
    half_dp = n_dp // 2
    path = d // half_dp
    block = d % half_dp
    c1 = path
    c2 = 1 - path
    chips = n_pipe // 2
    chip = p // 2
    core = p % 2
    relay = core == path
    other = p + 1 - 2 * core
    last = chips - 1
    k = chip + path * (last - 2 * chip)
    up = p + 2 - 4 * path
    down = p - 2 + 4 * path
    edge = (p == 0) | (p == n_pipe - 1)
    up_first = other + 2 - 4 * path
    half = w_in.shape[1] // 2
    piece = half // PIECES
    pieces = range(PIECES)
    pairs = ((c1, 2 + c1), (2 + c2, c2))
    share = 2 * half // n_dp
    cs = (c1, c2, c2, c1)

    def load(c):
        return (
            pltpu.make_async_copy(win_ref.at[0, c], w_in.at[c], w_sem.at[c, 0]),
            pltpu.make_async_copy(wout_ref.at[0, c], w_out.at[c], w_sem.at[c, 1]),
        )

    def lend(c):
        return [
            pltpu.make_async_remote_copy(
                src_ref=src.at[0, c],
                dst_ref=dst.at[2 + c],
                send_sem=share_send.at[c, n],
                recv_sem=share_recv.at[c, n],
                device_id={"pipe": other},
                device_id_type=MESH,
            )
            for n, (src, dst) in enumerate(((win_ref, w_in), (wout_ref, w_out)))
        ]

    start = pl.multiple_of(16 * (block // 2), 16)
    own_rows = pltpu.make_async_copy(cand_hbm.at[pl.ds(start, 16)], first_rows, cand_sem.at[0])
    all_rows = pltpu.make_async_copy(cand_hbm, cand_ref, cand_sem.at[1])

    id_copy = pltpu.make_async_copy(ids_hbm, ids_ref, cand_sem.at[2])

    @pl.when(relay & (k == 0))
    def _():
        own_rows.start()

    @pl.when(relay | (k == 0))
    def _():
        for copy in load(c1):
            copy.start()

    @pl.when(edge)
    def _():
        id_copy.start()

    @pl.when(relay)
    def _():
        for copy in load(c2):
            copy.start()

        @pl.when(k == 0)
        def _():
            all_rows.start()

    barrier = pltpu.get_barrier_semaphore()
    for to in (other, lax.rem(p + 2, n_pipe), lax.rem(p + n_pipe - 2, n_pipe)):
        pl.semaphore_signal(barrier, inc=1, device_id={"pipe": to}, device_id_type=MESH)

    def greet(n, carry):
        pl.semaphore_signal(
            barrier, inc=1, device_id={"dp": lax.rem(d + n, n_dp)}, device_id_type=MESH
        )
        return carry

    lax.fori_loop(1, n_dp, greet, 0)

    def far_first(n):
        side = d // 16, (d // 4) % 4, d % 4

        def away(t):
            return (2 + 3 * (t * (t + 1) // 2)) % 4

        plane = (side[0] + 1 - n % 2) % 2
        column = (side[1] + away(n // 8)) % 4
        return 16 * plane + 4 * column + (side[2] + away((n // 2) % 4)) % 4

    def piece_at(j):
        return pl.ds(j * piece, piece)

    def hop(ph, j, to):
        return pltpu.make_async_remote_copy(
            src_ref=give.at[ph, :, piece_at(j)],
            dst_ref=got.at[ph, :, piece_at(j)],
            send_sem=give_sem.at[ph, j],
            recv_sem=got_sem.at[ph, j],
            device_id={"pipe": to},
            device_id_type=MESH,
        )

    def back():
        return pltpu.make_async_remote_copy(
            src_ref=slopes.at[c1],
            dst_ref=slopes.at[2 + c1],
            send_sem=back_send,
            recv_sem=back_recv,
            device_id={"pipe": other},
            device_id_type=MESH,
        )

    def mail(ph):
        big = mid if ph in (0, 2) else got
        return [
            pltpu.make_async_remote_copy(
                src_ref=src,
                dst_ref=dst,
                send_sem=mail_send.at[ph, n],
                recv_sem=mail_recv.at[ph, n],
                device_id={"pipe": other},
                device_id_type=MESH,
            )
            for n, (src, dst) in enumerate(
                (
                    (big.at[ph], mail_big.at[ph]),
                    (small.at[ph, 1 if ph in (0, 2) else 0], mail_small.at[ph]),
                )
            )
        ]

    def spread_ids():
        id_copy.wait()
        lane = lax.broadcasted_iota(jnp.int32, (1, 128), 1)
        front = back = target = jnp.full((1, 128), -1, jnp.int32)
        ids_own[...] = jnp.full((8, 128), -1, jnp.int32)
        ids_own[0:5, 0:33] = ids_ref[...]
        plan = ids_own[4:5, :]
        for m in range(4):
            row = ids_own[m : m + 1, :]
            here = lane // 32 == m
            event = pltpu.roll(row, 32 * m, 1) if m else row
            is_front = plan[:, m : m + 1] < 2
            front = jnp.where(here & is_front, event, front)
            back = jnp.where(here & jnp.logical_not(is_front), event, back)
            target = jnp.where(here, pltpu.roll(row, (32 * m + 127) % 128, 1), target)
        ids_own[0:1, :] = front
        ids_own[1:2, :] = back
        ids_own[2:3, :] = target
        ids_all[d] = ids_own[...]

        def send(n, carry):
            pltpu.make_async_remote_copy(
                src_ref=ids_own,
                dst_ref=ids_all.at[d],
                send_sem=ids_send,
                recv_sem=ids_recv,
                device_id={"dp": lax.rem(d + n, n_dp)},
                device_id_type=MESH,
            ).start()
            return carry

        lax.fori_loop(1, n_dp, send, 0)

    def spread(ph, narrow, broad):
        c, kind = cs[ph], ph // 2
        narrow, broad = narrow[...], broad[...].astype(F32)
        hidden = narrow.shape[1] // 2
        top = jnp.concatenate([narrow[:, :hidden], narrow[:, hidden:]], axis=0).astype(BF16)
        wide = jnp.concatenate([broad, broad[:, :128]], axis=1)
        for j in range(half_dp):
            sbuf[c, kind, j, 0:16, :] = top
            sbuf[c, kind, j, 16:32, :] = wide[:, share * j : share * j + 128].astype(BF16)
        rbuf[c, kind, d] = sbuf[c, kind, block]

        def send(n, carry):
            peer = far_first(n)
            pltpu.make_async_remote_copy(
                src_ref=sbuf.at[c, kind, lax.rem(peer, half_dp)],
                dst_ref=rbuf.at[c, kind, d],
                send_sem=x_send.at[c, kind],
                recv_sem=x_recv.at[c, kind],
                device_id={"dp": peer},
                device_id_type=MESH,
            ).start()
            return carry

        lax.fori_loop(0, n_dp - 1, send, 0)

    def deliver(ph):
        if ph in (0, 2):
            spread(ph, small.at[ph, 0], got.at[ph])
        else:
            spread(ph, small.at[ph, 1], mid.at[ph])

    def many(ref, sem):
        return pltpu.make_async_copy(ref, ref, sem)

    def project(x2, j, weights, w, sums):
        low, high = sums
        low = low + mm(x2, weights[w, piece * j : piece * (j + 1), :])
        high = high + mm(x2, weights[w, half + piece * j : half + piece * (j + 1), :])
        return low, high

    def branch(parts, j):
        low = high = 0.0
        for narrow, weights, w in parts:
            low = low + mm(narrow, weights[w, :, piece * j : piece * (j + 1)])
            high = high + mm(narrow, weights[w, :, half + piece * j : half + piece * (j + 1)])
        return jnp.concatenate([low[:8], high[8:]], axis=0)

    def add_branch(out, ph, x, parts, sent=None):
        for j in pieces:
            at = piece_at(j)
            out[ph, :, at] = (x[ph, :, at].astype(F32) + branch(parts, j)).astype(BF16)
            if sent is not None:
                sent(j)

    def activate(pre, w):
        logistic = 1.0 / (1.0 + jnp.exp(-pre))
        slopes[w] = logistic * (1.0 + pre * (1.0 - logistic))
        return pre * logistic

    def nothing():
        zeros = jnp.zeros((16, w_in.shape[2]), F32)
        return zeros, zeros

    def gather(sums):
        return sums[0][:8] + sums[1][8:]

    def forward_one(x, n, w):
        sums = nothing()
        for j in pieces:
            sums = project(x[n, :, piece_at(j)], j, w_in, w, sums)
        return activate(gather(sums), w)

    def forward_pair(ph, arrived, sent):
        a, b = pairs[ph]
        sums_a, sums_b = nothing(), nothing()
        for j in pieces:
            arrived(j)
            x2 = got[ph, :, piece_at(j)]
            sums_a = project(x2, j, w_in, a, sums_a)
            sums_b = project(x2, j, w_in, b, sums_b)
        act_a = activate(gather(sums_a), a)
        small[ph, 0] = act_a
        act_a = twice(act_a)
        act_b = activate(gather(sums_b) + mm(act_a, m_fwd[ph])[:8], b)
        small[ph, 1] = act_b
        parts = [(act_a, w_out, a), (twice(act_b), w_out, b)]
        add_branch(give, ph, got, parts, sent)
        return parts

    def backward_pair(ph, arrived):
        a, b = pairs[3 - ph]
        sums_a, sums_b = nothing(), nothing()
        for j in pieces:
            arrived(j)
            g2 = got[ph, :, piece_at(j)]
            sums_b = project(g2, j, t_out, b, sums_b)
            sums_a = project(g2, j, t_out, a, sums_a)
        grad_b = gather(sums_b) * slopes[b]
        small[ph, 0] = grad_b
        grad_b = twice(grad_b)
        grad_a = (gather(sums_a) + mm(grad_b, m_bwd[3 - ph])[:8]) * slopes[a]
        small[ph, 1] = grad_a
        return [(grad_b, t_in, b), (twice(grad_a), t_in, a)]

    def between(blk):
        a, b = pairs[blk]
        both = mm(w_out[a], w_in[b])
        m_fwd[blk] = both.astype(BF16)
        m_bwd[blk] = both.T.astype(BF16)

    def turn():
        tile = w_in.shape[2]

        def one(n, carry):
            w, at = n // (2 * half // tile), n % (2 * half // tile)
            at = pl.ds(pl.multiple_of(at * tile, tile), tile)
            t_in[w, :, at] = w_in[w, at, :].T
            t_out[w, at, :] = w_out[w, :, at].T
            return carry

        lax.fori_loop(0, 4 * (2 * half // tile), one, 0)

    def unpack(c, kind):
        many(rbuf.at[c, kind, pl.ds(0, n_dp - 1)], x_recv.at[c, kind]).wait()
        rows = rbuf[c, kind].astype(F32)
        flat = lambda part: part.reshape(n_dp * 8, 128)
        narrow = jnp.concatenate([flat(rows[:, 0:8]), flat(rows[:, 8:16])], axis=1)
        broad = jnp.where(path == 0, flat(rows[:, 16:24]), flat(rows[:, 24:32]))
        return narrow.astype(BF16), broad

    def prepare():
        for c in (0, 1):
            act, x = unpack(c, 0)
            act_rows[c] = act
            x_turned[c] = x.T.astype(BF16)

    def finish(c):
        grad_pre, grad_y = unpack(c, 1)
        gin_ref[0, c] = mm(x_turned[c], grad_pre)[:share]
        gout_ref[0, c] = mm(grad_y.T.astype(BF16), act_rows[c])[:share]

    early = 1 - chip // (chips // 2)

    def seeds():
        all_rows.wait()
        own = lax.broadcasted_iota(jnp.int32, (16, 128), 0) + 8 * block
        every = lax.broadcasted_iota(jnp.int32, (128, 128), 0)

        def count(group, total):
            left, right = [], []
            for n in range(8):
                tile = ids_all[group * 8 + n]
                events = jnp.where(path == 0, tile[0:1, :], tile[1:2, :])
                left.append(jnp.where(own == events, 1.0, 0.0).astype(BF16))
                right.append(jnp.where(every == tile[2:3, :], 1.0, 0.0).astype(BF16))
            return total + mm_t(jnp.concatenate(left, axis=1), jnp.concatenate(right, axis=1))

        counts = lax.fori_loop(0, n_dp // 8, count, jnp.zeros((16, 128), F32))[:8]
        sixteens = jnp.floor(counts * 0.0625)
        parts = jnp.concatenate([sixteens, counts - 16.0 * sixteens], axis=0).astype(BF16)
        sums = mm(parts, cand_ref[...])
        got[2] = fold((16.0 * sums[:8] + sums[8:]) * scale).astype(BF16)

    @pl.when(relay & (k == 0))
    def _():
        own_rows.wait()
        rows = first_rows[...].astype(F32)
        mine = jnp.where(block % 2 == 0, rows[:8], rows[8:])
        got[0] = fold(mine).astype(BF16)
        for copy in load(c1):
            copy.wait()
        act = forward_one(got, 0, c1)
        small[0, 0] = act
        add_branch(mid, 0, got, [(twice(act), w_out, c1)])

    pl.semaphore_wait(barrier, n_dp + 2)

    @pl.when(jnp.logical_not(relay))
    def _():
        @pl.when(k == 0)
        def _():
            for copy in load(c1):
                copy.wait()
            mail(0)[0].wait_recv()
            act = forward_one(mail_big, 0, c1)
            mail_small[0] = act
            add_branch(
                give,
                0,
                mail_big,
                [(twice(act), w_out, c1)],
                lambda j: hop(0, j, up_first).start(),
            )
            back().start()

        for copy in lend(c1):
            copy.start()

        @pl.when(edge)
        def _():
            spread_ids()

        for copy in lend(c1):
            copy.wait_send()
        for copy in lend(c2):
            copy.start()

        @pl.when(k > 0)
        def _():
            for copy in mail(0):
                copy.wait_recv()

        spread(0, mail_small.at[0], mail_big.at[0])
        for ph in (1, 2):
            for copy in mail(ph):
                copy.wait_recv()
            spread(ph, mail_small.at[ph], mail_big.at[ph])
        prepare()

        @pl.when(k == 0)
        def _():
            finish(early)

        for copy in mail(3):
            copy.wait_recv()
        spread(3, mail_small.at[3], mail_big.at[3])

        @pl.when(k > 0)
        def _():
            finish(early)

        finish(1 - early)
        for copy in lend(c2):
            copy.wait_send()

        @pl.when(k == 0)
        def _():
            for j in pieces:
                hop(0, j, up_first).wait_send()
            back().wait_send()

        @pl.when(edge)
        def _():
            many(ids_all.at[pl.ds(0, n_dp - 1)], ids_recv).wait()

    @pl.when(relay)
    def _():
        def from_below(ph):
            def wait(j):
                @pl.when(k > 0)
                def _():
                    hop(ph, j, down).wait_recv()

            return wait

        def from_above(ph):
            def wait(j):
                @pl.when(k < last)
                def _():
                    hop(ph, j, up).wait_recv()

            return wait

        def to_above(ph):
            def send(j):
                @pl.when(k < last)
                def _():
                    hop(ph, j, up).start()

            return send

        def to_below(ph):
            def send(j):
                @pl.when(k > 0)
                def _():
                    hop(ph, j, down).start()

            return send

        def lent(blk):
            for copy in lend((c1, c2)[blk]):
                copy.wait_recv()

        def post(ph):
            for copy in mail(ph):
                copy.start()

        @pl.when(k == 0)
        def _():
            mail(0)[0].start()
            spread_ids()
            deliver(0)
            lent(0)
            between(0)
            for copy in load(c2):
                copy.wait()
            lent(1)
            between(1)
            turn()
            many(ids_all.at[pl.ds(0, n_dp - 1)], ids_recv).wait()
            seeds()
            back().wait_recv()

        @pl.when(k > 0)
        def _():
            for copy in load(c1):
                copy.wait()
            lent(0)
            between(0)

            @pl.when(k == last)
            def _():
                for copy in load(c2):
                    copy.wait()
                lent(1)
                between(1)

            parts = forward_pair(0, from_below(0), to_above(0))
            add_branch(mid, 0, got, parts[:1])
            post(0)

            @pl.when(k == last)
            def _():
                got[1] = give[0]

            @pl.when(k < last)
            def _():
                deliver(0)
                for copy in load(c2):
                    copy.wait()
                lent(1)
                between(1)

                @pl.when(k < chips // 2)
                def _():
                    turn()

        parts = forward_pair(1, from_above(1), to_below(1))
        post(1)
        add_branch(mid, 1, got, parts[:1])

        @pl.when(k > 0)
        def _():
            deliver(1)

            @pl.when(k == last)
            def _():
                deliver(0)

            @pl.when(k >= chips // 2)
            def _():
                turn()

        parts = backward_pair(2, from_below(2))
        add_branch(give, 2, got, parts, to_above(2))
        add_branch(mid, 2, got, parts[:1])
        post(2)

        @pl.when(k < last)
        def _():
            @pl.when(k == 0)
            def _():
                deliver(1)

            deliver(2)
            prepare()

            @pl.when(k == 0)
            def _():
                finish(early)

        @pl.when(k == last)
        def _():
            got[3] = give[2]

        parts = backward_pair(3, from_above(3))

        @pl.when(k > 0)
        def _():
            add_branch(give, 3, got, parts, to_below(3))

        post(3)
        add_branch(mid, 3, got, parts[:1])
        deliver(3)

        @pl.when(k == last)
        def _():
            deliver(2)
            prepare()

        @pl.when(k > 0)
        def _():
            finish(early)

        finish(1 - early)

        @pl.when(k < last)
        def _():
            for j in pieces:
                hop(2, j, up).wait_send()

        @pl.when((k > 0) & (k < last))
        def _():
            for j in pieces:
                hop(0, j, up).wait_send()

        @pl.when(k > 0)
        def _():
            for j in pieces:
                hop(1, j, down).wait_send()
                hop(3, j, down).wait_send()
            mail(0)[1].wait_send()

        mail(0)[0].wait_send()
        for ph in (1, 2, 3):
            for copy in mail(ph):
                copy.wait_send()

    @pl.when(edge)
    def _():
        many(ids_all.at[pl.ds(0, n_dp - 1)], ids_send).wait()

    for c in (0, 1):
        for kind in (0, 1):
            many(rbuf.at[c, kind, pl.ds(0, n_dp - 1)], x_send.at[c, kind]).wait()


def local(n_pipe, n_dp, item_ids, plan_order, candidates, adapters_in, adapters_out):
    batches, width = item_ids.shape
    events = width - 1
    _, _, features, hidden = adapters_in.shape
    share = features // n_dp
    scale = 1.0 / math.sqrt(batches * n_dp * events)
    plan = jnp.pad(plan_order, (0, item_ids.shape[1] - plan_order.shape[0]))
    ids = jnp.concatenate([item_ids, plan[None]], axis=0)
    vmem = pl.BlockSpec(memory_space=pltpu.VMEM)
    hbm = pl.BlockSpec(memory_space=pltpu.HBM)
    grad_in, grad_out = pl.pallas_call(
        functools.partial(kernel, n_pipe, n_dp, scale),
        out_shape=(
            jax.ShapeDtypeStruct((1, 2, share, hidden), F32),
            jax.ShapeDtypeStruct((1, 2, share, hidden), F32),
        ),
        in_specs=[hbm] * 4,
        out_specs=(vmem, vmem),
        scratch_shapes=[
            pltpu.VMEM((4, features, hidden), BF16),
            pltpu.VMEM((4, hidden, features), BF16),
            pltpu.VMEM((4, hidden, features), BF16),
            pltpu.VMEM((4, features, hidden), BF16),
            pltpu.VMEM((2, hidden, hidden), BF16),
            pltpu.VMEM((2, hidden, hidden), BF16),
            pltpu.VMEM(ids.shape, jnp.int32),
            pltpu.VMEM(candidates.shape, BF16),
            pltpu.VMEM((16, features), BF16),
            pltpu.VMEM((8, 128), jnp.int32),
            pltpu.VMEM((n_dp, 8, 128), jnp.int32),
            pltpu.VMEM((4, 16, features // 2), BF16),
            pltpu.VMEM((4, 16, features // 2), BF16),
            pltpu.VMEM((4, 16, features // 2), BF16),
            pltpu.VMEM((4, 2, 8, hidden), F32),
            pltpu.VMEM((4, 8, hidden), F32),
            pltpu.VMEM((4, 16, features // 2), BF16),
            pltpu.VMEM((4, 8, hidden), F32),
            pltpu.VMEM((2, 2, n_dp // 2, 32, 128), BF16),
            pltpu.VMEM((2, 2, n_dp, 32, 128), BF16),
            pltpu.VMEM((2, 128, n_dp * 8), BF16),
            pltpu.VMEM((2, n_dp * 8, hidden), BF16),
            pltpu.SemaphoreType.DMA((2, 2)),
            pltpu.SemaphoreType.DMA((3,)),
            pltpu.SemaphoreType.DMA((2, 2)),
            pltpu.SemaphoreType.DMA((2, 2)),
            pltpu.SemaphoreType.DMA((4, PIECES)),
            pltpu.SemaphoreType.DMA((4, PIECES)),
            pltpu.SemaphoreType.DMA((4, 2)),
            pltpu.SemaphoreType.DMA((4, 2)),
            pltpu.SemaphoreType.DMA,
            pltpu.SemaphoreType.DMA,
            pltpu.SemaphoreType.DMA,
            pltpu.SemaphoreType.DMA,
            pltpu.SemaphoreType.DMA((2, 2)),
            pltpu.SemaphoreType.DMA((2, 2)),
        ],
        compiler_params=pltpu.CompilerParams(
            collective_id=0, has_side_effects=True, vmem_limit_bytes=107 * 512 * 1024
        ),
    )(ids, candidates, adapters_in, adapters_out)
    return grad_in, jnp.swapaxes(grad_out, 2, 3)


def solution(mesh):
    in_specs = (P(None, "dp"), P(), P(), P("pipe", None, None, None), P("pipe", None, None, None))
    out_specs = (P("pipe", None, "dp", None), P("pipe", None, None, "dp"))
    return jax.shard_map(
        functools.partial(local, mesh.shape["pipe"], mesh.shape["dp"]),
        mesh=mesh,
        in_specs=in_specs,
        out_specs=out_specs,
        check_vma=False,
    )
```

time: 108 us -> 80.6 us (0.75)
  Pallas kernels: 98.6 us -> 75.8 us
  local copies, waits for them, and re-layouts: 6.72 us -> 2.01 us
    pallas_call x1, Pallas kernels: 98.6 us -> 75.8 us  [local(): pl.pallas_call(functools.partial(kernel, n_pipe, n_dp, scale), out_shape=...]
    unnamed x7 -> x2, local copies, waits for them, and re-layouts: 5.59 us -> 1.36 us
where the time goes in v2:
time: 80.6 us; the launch traced here: 79.1 us
  Pallas kernels  75.8 us (94%)
  local copies, waits for them, and re-layouts  2.01 us (2%)
    pallas_call x1, Pallas kernels, local(): pl.pallas_call(functools.partial(kernel, n_pipe, n_dp, scale), out_shape=...  75.8 us

profile of v2, /device:TPU:32, one launch (start us, length us, event | category | flops | bytes accessed | tf_op | source)
XLA Modules:
  0.0 79.1 jit_solution(5570926084374076800)
XLA Ops:
  0.6 0.7 pad_bitcast_fusion
  1.3 0.7 pad_add_fusion.ids_hbm
  2.0 75.8 %shard_map.68 = (f32[1,2,96,256]{3,2,1,0:T(8,128)S(1)}, f32[1,2,96,256]{3,2,1,0:T(8,128)S(1)}) custom-call(s32[5,33]{1,0:T(8,128)S(1)} %pad_add_fusion.ids_hbm, bf16[128,3072]{1,0:T(8,128)(2,1)} %cand_hbm.1, bf16[1,2,3072,256]{3,2,1,0:T(8,128)(2,1)} %win_ref.1, bf16[1,2,256,3072]{3,2,1,0:T(8,128)(2,1)} %wout_ref.1), custom_call_target="tpu_custom_call" | custom-call | tf_op jit(solution)/shard_map/pallas_call | solution.py:691
  77.7 0.7 copy.9
  78.4 0.7 copy.10

commit v3 on v2

--- a/solution.py
+++ b/solution.py
@@ -56,13 +56,10 @@
     first_rows,
     ids_own,
     ids_all,
-    got,
-    mid,
+    xs,
     give,
     small,
     slopes,
-    mail_big,
-    mail_small,
     sbuf,
     rbuf,
     x_turned,
@@ -75,6 +72,8 @@
     got_sem,
     mail_send,
     mail_recv,
+    pass_send,
+    pass_recv,
     back_send,
     back_recv,
     ids_send,
@@ -92,18 +91,23 @@
     chips = n_pipe // 2
     chip = p // 2
     core = p % 2
-    relay = core == path
+    relay = core == 1
+    starts = core == path
     other = p + 1 - 2 * core
     last = chips - 1
     k = chip + path * (last - 2 * chip)
-    up = p + 2 - 4 * path
-    down = p - 2 + 4 * path
-    edge = (p == 0) | (p == n_pipe - 1)
-    up_first = other + 2 - 4 * path
+    up = 2 * chip + 3 - 4 * path
+    down = 2 * chip - 1 + 4 * path
+    edge = (k == 0) | (k == last)
     half = w_in.shape[1] // 2
+    n_items = cand_ref.shape[0]
     piece = half // PIECES
     pieces = range(PIECES)
-    pairs = ((c1, 2 + c1), (2 + c2, c2))
+    pairs = ((c1 + 2 - 2 * path, c1 + 2 * path), (c2 + 2 * path, c2 + 2 - 2 * path))
+
+    def own(ph):
+        return (ph + 1 + path) % 2
+
     share = 2 * half // n_dp
     cs = (c1, c2, c2, c1)
 
@@ -132,7 +136,7 @@
 
     id_copy = pltpu.make_async_copy(ids_hbm, ids_ref, cand_sem.at[2])
 
-    @pl.when(relay & (k == 0))
+    @pl.when(starts & (k == 0))
     def _():
         own_rows.start()
 
@@ -141,12 +145,12 @@
         for copy in load(c1):
             copy.start()
 
-    @pl.when(edge)
-    def _():
-        id_copy.start()
-
     @pl.when(relay)
     def _():
+        @pl.when(edge)
+        def _():
+            id_copy.start()
+
         for copy in load(c2):
             copy.start()
 
@@ -155,8 +159,19 @@
             all_rows.start()
 
     barrier = pltpu.get_barrier_semaphore()
-    for to in (other, lax.rem(p + 2, n_pipe), lax.rem(p + n_pipe - 2, n_pipe)):
+
+    def hello(to):
         pl.semaphore_signal(barrier, inc=1, device_id={"pipe": to}, device_id_type=MESH)
+
+    hello(other)
+
+    @pl.when(relay & (k < last))
+    def _():
+        hello(up)
+
+    @pl.when(relay & (k > 0))
+    def _():
+        hello(down)
 
     def greet(n, carry):
         pl.semaphore_signal(
@@ -182,7 +197,7 @@
     def hop(ph, j, to):
         return pltpu.make_async_remote_copy(
             src_ref=give.at[ph, :, piece_at(j)],
-            dst_ref=got.at[ph, :, piece_at(j)],
+            dst_ref=xs.at[ph, 0, :, piece_at(j)],
             send_sem=give_sem.at[ph, j],
             recv_sem=got_sem.at[ph, j],
             device_id={"pipe": to},
@@ -199,23 +214,28 @@
             device_id_type=MESH,
         )
 
+    def pass_on():
+        return pltpu.make_async_remote_copy(
+            src_ref=xs.at[0, 1],
+            dst_ref=xs.at[0, 1],
+            send_sem=pass_send,
+            recv_sem=pass_recv,
+            device_id={"pipe": other},
+            device_id_type=MESH,
+        )
+
     def mail(ph):
-        big = mid if ph in (0, 2) else got
+        n = 1 - own(ph)
         return [
             pltpu.make_async_remote_copy(
-                src_ref=src,
-                dst_ref=dst,
-                send_sem=mail_send.at[ph, n],
-                recv_sem=mail_recv.at[ph, n],
+                src_ref=ref.at[ph, n],
+                dst_ref=ref.at[ph, n],
+                send_sem=mail_send.at[ph, m],
+                recv_sem=mail_recv.at[ph, m],
                 device_id={"pipe": other},
                 device_id_type=MESH,
             )
-            for n, (src, dst) in enumerate(
-                (
-                    (big.at[ph], mail_big.at[ph]),
-                    (small.at[ph, 1 if ph in (0, 2) else 0], mail_small.at[ph]),
-                )
-            )
+            for m, ref in enumerate((xs, small))
         ]
 
     def spread_ids():
@@ -223,15 +243,17 @@
         lane = lax.broadcasted_iota(jnp.int32, (1, 128), 1)
         front = back = target = jnp.full((1, 128), -1, jnp.int32)
         ids_own[...] = jnp.full((8, 128), -1, jnp.int32)
-        ids_own[0:5, 0:33] = ids_ref[...]
-        plan = ids_own[4:5, :]
+        ids_own[0:4, 0:33] = ids_ref[...]
         for m in range(4):
             row = ids_own[m : m + 1, :]
+            is_front = row < 2 * n_items
+            for above in (2 * n_items, n_items):
+                row = jnp.where(row >= above, row - above, row)
+            fronts = jnp.where(is_front, row, -1)
+            backs = jnp.where(is_front, -1, row)
             here = lane // 32 == m
-            event = pltpu.roll(row, 32 * m, 1) if m else row
-            is_front = plan[:, m : m + 1] < 2
-            front = jnp.where(here & is_front, event, front)
-            back = jnp.where(here & jnp.logical_not(is_front), event, back)
+            front = jnp.where(here, pltpu.roll(fronts, 32 * m, 1) if m else fronts, front)
+            back = jnp.where(here, pltpu.roll(backs, 32 * m, 1) if m else backs, back)
             target = jnp.where(here, pltpu.roll(row, (32 * m + 127) % 128, 1), target)
         ids_own[0:1, :] = front
         ids_own[1:2, :] = back
@@ -276,11 +298,8 @@
 
         lax.fori_loop(0, n_dp - 1, send, 0)
 
-    def deliver(ph):
-        if ph in (0, 2):
-            spread(ph, small.at[ph, 0], got.at[ph])
-        else:
-            spread(ph, small.at[ph, 1], mid.at[ph])
+    def deliver(ph, n):
+        spread(ph, small.at[ph, n], xs.at[ph, n])
 
     def many(ref, sem):
         return pltpu.make_async_copy(ref, ref, sem)
@@ -298,10 +317,10 @@
             high = high + mm(narrow, weights[w, :, half + piece * j : half + piece * (j + 1)])
         return jnp.concatenate([low[:8], high[8:]], axis=0)
 
-    def add_branch(out, ph, x, parts, sent=None):
+    def add_branch(out, x, parts, sent=None):
         for j in pieces:
             at = piece_at(j)
-            out[ph, :, at] = (x[ph, :, at].astype(F32) + branch(parts, j)).astype(BF16)
+            out[:, at] = (x[:, at].astype(F32) + branch(parts, j)).astype(BF16)
             if sent is not None:
                 sent(j)
 
@@ -317,18 +336,20 @@
     def gather(sums):
         return sums[0][:8] + sums[1][8:]
 
-    def forward_one(x, n, w):
+    def forward_one(n):
         sums = nothing()
         for j in pieces:
-            sums = project(x[n, :, piece_at(j)], j, w_in, w, sums)
-        return activate(gather(sums), w)
+            sums = project(xs[0, n, :, piece_at(j)], j, w_in, c1, sums)
+        act = activate(gather(sums), c1)
+        small[0, n] = act
+        return [(twice(act), w_out, c1)]
 
     def forward_pair(ph, arrived, sent):
         a, b = pairs[ph]
         sums_a, sums_b = nothing(), nothing()
         for j in pieces:
             arrived(j)
-            x2 = got[ph, :, piece_at(j)]
+            x2 = xs[ph, 0, :, piece_at(j)]
             sums_a = project(x2, j, w_in, a, sums_a)
             sums_b = project(x2, j, w_in, b, sums_b)
         act_a = activate(gather(sums_a), a)
@@ -337,7 +358,7 @@
         act_b = activate(gather(sums_b) + mm(act_a, m_fwd[ph])[:8], b)
         small[ph, 1] = act_b
         parts = [(act_a, w_out, a), (twice(act_b), w_out, b)]
-        add_branch(give, ph, got, parts, sent)
+        add_branch(give.at[ph], xs.at[ph, 0], parts, sent)
         return parts
 
     def backward_pair(ph, arrived):
@@ -345,7 +366,7 @@
         sums_a, sums_b = nothing(), nothing()
         for j in pieces:
             arrived(j)
-            g2 = got[ph, :, piece_at(j)]
+            g2 = xs[ph, 0, :, piece_at(j)]
             sums_b = project(g2, j, t_out, b, sums_b)
             sums_a = project(g2, j, t_out, a, sums_a)
         grad_b = gather(sums_b) * slopes[b]
@@ -396,7 +417,7 @@
 
     def seeds():
         all_rows.wait()
-        own = lax.broadcasted_iota(jnp.int32, (16, 128), 0) + 8 * block
+        mine = lax.broadcasted_iota(jnp.int32, (16, 128), 0) + 8 * block
         every = lax.broadcasted_iota(jnp.int32, (128, 128), 0)
 
         def count(group, total):
@@ -404,7 +425,7 @@
             for n in range(8):
                 tile = ids_all[group * 8 + n]
                 events = jnp.where(path == 0, tile[0:1, :], tile[1:2, :])
-                left.append(jnp.where(own == events, 1.0, 0.0).astype(BF16))
+                left.append(jnp.where(mine == events, 1.0, 0.0).astype(BF16))
                 right.append(jnp.where(every == tile[2:3, :], 1.0, 0.0).astype(BF16))
             return total + mm_t(jnp.concatenate(left, axis=1), jnp.concatenate(right, axis=1))
 
@@ -412,47 +433,53 @@
         sixteens = jnp.floor(counts * 0.0625)
         parts = jnp.concatenate([sixteens, counts - 16.0 * sixteens], axis=0).astype(BF16)
         sums = mm(parts, cand_ref[...])
-        got[2] = fold((16.0 * sums[:8] + sums[8:]) * scale).astype(BF16)
-
-    @pl.when(relay & (k == 0))
+        xs[2, 0] = fold((16.0 * sums[:8] + sums[8:]) * scale).astype(BF16)
+
+    @pl.when(starts & (k == 0))
     def _():
         own_rows.wait()
         rows = first_rows[...].astype(F32)
         mine = jnp.where(block % 2 == 0, rows[:8], rows[8:])
-        got[0] = fold(mine).astype(BF16)
+        xs[0, 0] = fold(mine).astype(BF16)
         for copy in load(c1):
             copy.wait()
-        act = forward_one(got, 0, c1)
-        small[0, 0] = act
-        add_branch(mid, 0, got, [(twice(act), w_out, c1)])
-
-    pl.semaphore_wait(barrier, n_dp + 2)
+        add_branch(xs.at[0, 1], xs.at[0, 0], forward_one(0))
+
+    @pl.when(relay & (k > 0) & (k < last))
+    def _():
+        pl.semaphore_wait(barrier, n_dp + 2)
+
+    @pl.when(relay & edge)
+    def _():
+        pl.semaphore_wait(barrier, n_dp + 1)
 
     @pl.when(jnp.logical_not(relay))
     def _():
-        @pl.when(k == 0)
+        pl.semaphore_wait(barrier, n_dp)
+
+    @pl.when(k == 0)
+    def _():
+        @pl.when(starts)
+        def _():
+            pass_on().start()
+
+        @pl.when(jnp.logical_not(starts))
         def _():
             for copy in load(c1):
                 copy.wait()
-            mail(0)[0].wait_recv()
-            act = forward_one(mail_big, 0, c1)
-            mail_small[0] = act
+            pass_on().wait_recv()
             add_branch(
-                give,
-                0,
-                mail_big,
-                [(twice(act), w_out, c1)],
-                lambda j: hop(0, j, up_first).start(),
+                give.at[0], xs.at[0, 1], forward_one(1), lambda j: hop(0, j, up).start()
             )
+
+    @pl.when(jnp.logical_not(relay))
+    def _():
+        @pl.when(k == 0)
+        def _():
             back().start()
 
         for copy in lend(c1):
             copy.start()
-
-        @pl.when(edge)
-        def _():
-            spread_ids()
-
         for copy in lend(c1):
             copy.wait_send()
         for copy in lend(c2):
@@ -463,11 +490,11 @@
             for copy in mail(0):
                 copy.wait_recv()
 
-        spread(0, mail_small.at[0], mail_big.at[0])
+        deliver(0, 1 - own(0))
         for ph in (1, 2):
             for copy in mail(ph):
                 copy.wait_recv()
-            spread(ph, mail_small.at[ph], mail_big.at[ph])
+            deliver(ph, 1 - own(ph))
         prepare()
 
         @pl.when(k == 0)
@@ -476,7 +503,7 @@
 
         for copy in mail(3):
             copy.wait_recv()
-        spread(3, mail_small.at[3], mail_big.at[3])
+        deliver(3, 1 - own(3))
 
         @pl.when(k > 0)
         def _():
@@ -488,13 +515,7 @@
 
         @pl.when(k == 0)
         def _():
-            for j in pieces:
-                hop(0, j, up_first).wait_send()
             back().wait_send()
-
-        @pl.when(edge)
-        def _():
-            many(ids_all.at[pl.ds(0, n_dp - 1)], ids_recv).wait()
 
     @pl.when(relay)
     def _():
@@ -540,9 +561,8 @@
 
         @pl.when(k == 0)
         def _():
-            mail(0)[0].start()
             spread_ids()
-            deliver(0)
+            deliver(0, own(0))
             lent(0)
             between(0)
             for copy in load(c2):
@@ -563,22 +583,23 @@
 
             @pl.when(k == last)
             def _():
+                spread_ids()
                 for copy in load(c2):
                     copy.wait()
                 lent(1)
                 between(1)
 
             parts = forward_pair(0, from_below(0), to_above(0))
-            add_branch(mid, 0, got, parts[:1])
+            add_branch(xs.at[0, 1], xs.at[0, 0], parts[:1])
             post(0)
 
             @pl.when(k == last)
             def _():
-                got[1] = give[0]
+                xs[1, 0] = give[0]
 
             @pl.when(k < last)
             def _():
-                deliver(0)
+                deliver(0, own(0))
                 for copy in load(c2):
                     copy.wait()
                 lent(1)
@@ -589,33 +610,33 @@
                     turn()
 
         parts = forward_pair(1, from_above(1), to_below(1))
+        add_branch(xs.at[1, 1], xs.at[1, 0], parts[:1])
         post(1)
-        add_branch(mid, 1, got, parts[:1])
 
         @pl.when(k > 0)
         def _():
-            deliver(1)
+            deliver(1, own(1))
 
             @pl.when(k == last)
             def _():
-                deliver(0)
+                deliver(0, own(0))
 
             @pl.when(k >= chips // 2)
             def _():
                 turn()
 
         parts = backward_pair(2, from_below(2))
-        add_branch(give, 2, got, parts, to_above(2))
-        add_branch(mid, 2, got, parts[:1])
+        add_branch(give.at[2], xs.at[2, 0], parts, to_above(2))
+        add_branch(xs.at[2, 1], xs.at[2, 0], parts[:1])
         post(2)
 
         @pl.when(k < last)
         def _():
             @pl.when(k == 0)
             def _():
-                deliver(1)
-
-            deliver(2)
+                deliver(1, own(1))
+
+            deliver(2, own(2))
             prepare()
 
             @pl.when(k == 0)
@@ -624,21 +645,21 @@
 
         @pl.when(k == last)
         def _():
-            got[3] = give[2]
+            xs[3, 0] = give[2]
 
         parts = backward_pair(3, from_above(3))
 
         @pl.when(k > 0)
         def _():
-            add_branch(give, 3, got, parts, to_below(3))
-
+            add_branch(give.at[3], xs.at[3, 0], parts, to_below(3))
+
+        add_branch(xs.at[3, 1], xs.at[3, 0], parts[:1])
         post(3)
-        add_branch(mid, 3, got, parts[:1])
-        deliver(3)
+        deliver(3, own(3))
 
         @pl.when(k == last)
         def _():
-            deliver(2)
+            deliver(2, own(2))
             prepare()
 
         @pl.when(k > 0)
@@ -662,16 +683,31 @@
             for j in pieces:
                 hop(1, j, down).wait_send()
                 hop(3, j, down).wait_send()
-            mail(0)[1].wait_send()
-
-        mail(0)[0].wait_send()
+            for copy in mail(0):
+                copy.wait_send()
+
         for ph in (1, 2, 3):
             for copy in mail(ph):
                 copy.wait_send()
 
-    @pl.when(edge)
-    def _():
-        many(ids_all.at[pl.ds(0, n_dp - 1)], ids_send).wait()
+        @pl.when(k == last)
+        def _():
+            many(ids_all.at[pl.ds(0, n_dp - 1)], ids_recv).wait()
+
+        @pl.when(edge)
+        def _():
+            many(ids_all.at[pl.ds(0, n_dp - 1)], ids_send).wait()
+
+    @pl.when(k == 0)
+    def _():
+        @pl.when(starts)
+        def _():
+            pass_on().wait_send()
+
+        @pl.when(jnp.logical_not(starts))
+        def _():
+            for j in pieces:
+                hop(0, j, up).wait_send()
 
     for c in (0, 1):
         for kind in (0, 1):
@@ -684,8 +720,7 @@
     _, _, features, hidden = adapters_in.shape
     share = features // n_dp
     scale = 1.0 / math.sqrt(batches * n_dp * events)
-    plan = jnp.pad(plan_order, (0, item_ids.shape[1] - plan_order.shape[0]))
-    ids = jnp.concatenate([item_ids, plan[None]], axis=0)
+    ids = item_ids + candidates.shape[0] * plan_order[:, None]
     vmem = pl.BlockSpec(memory_space=pltpu.VMEM)
     hbm = pl.BlockSpec(memory_space=pltpu.HBM)
     grad_in, grad_out = pl.pallas_call(
@@ -708,12 +743,9 @@
             pltpu.VMEM((16, features), BF16),
             pltpu.VMEM((8, 128), jnp.int32),
             pltpu.VMEM((n_dp, 8, 128), jnp.int32),
-            pltpu.VMEM((4, 16, features // 2), BF16),
-            pltpu.VMEM((4, 16, features // 2), BF16),
+            pltpu.VMEM((4, 2, 16, features // 2), BF16),
             pltpu.VMEM((4, 16, features // 2), BF16),
             pltpu.VMEM((4, 2, 8, hidden), F32),
-            pltpu.VMEM((4, 8, hidden), F32),
-            pltpu.VMEM((4, 16, features // 2), BF16),
             pltpu.VMEM((4, 8, hidden), F32),
             pltpu.VMEM((2, 2, n_dp // 2, 32, 128), BF16),
             pltpu.VMEM((2, 2, n_dp, 32, 128), BF16),
@@ -731,6 +763,8 @@
             pltpu.SemaphoreType.DMA,
             pltpu.SemaphoreType.DMA,
             pltpu.SemaphoreType.DMA,
+            pltpu.SemaphoreType.DMA,
+            pltpu.SemaphoreType.DMA,
             pltpu.SemaphoreType.DMA((2, 2)),
             pltpu.SemaphoreType.DMA((2, 2)),
         ],

time: 80.6 us -> 71.6 us (0.89); the launches traced: 79.1 us -> 71.3 us
  Pallas kernels: 75.8 us -> 67.9 us
    pallas_call x1, Pallas kernels: 75.8 us -> 67.9 us  [local(): pl.pallas_call(functools.partial(kernel, n_pipe, n_dp, scale), out_shape=...]
where the time goes in v3:
time: 71.6 us; the launch traced here: 71.3 us
  Pallas kernels  67.9 us (95%)
  other arithmetic  1.41 us (2%)
  local copies, waits for them, and re-layouts  1.36 us (2%)
    pallas_call x1, Pallas kernels, local(): pl.pallas_call(functools.partial(kernel, n_pipe, n_dp, scale), out_shape=...  67.9 us

profile of v3, /device:TPU:32, one launch (start us, length us, event | category | flops | bytes accessed | tf_op | source)
XLA Modules:
  0.0 71.3 jit_solution(15217717120309464852)
XLA Ops:
  0.6 0.7 broadcast_multiply_fusion
  1.3 0.8 %broadcast_add_fusion.ids_hbm = s32[4,33]{1,0:T(4,128)S(1)} fusion(s32[4,33]{1,0:T(4,128)} %param.5, s32[4]{0:T(128)S(1)} %broadcast_multiply_fusion), kind=kLoop, calls=%fused_computation | loop fusion | flops 132 | bytes 1072 | tf_op jit(solution)/shard_map/add | solution.py:723
  2.0 67.9 %shard_map.68 = (f32[1,2,96,256]{3,2,1,0:T(8,128)S(1)}, f32[1,2,96,256]{3,2,1,0:T(8,128)S(1)}) custom-call(s32[4,33]{1,0:T(4,128)S(1)} %broadcast_add_fusion.ids_hbm, bf16[128,3072]{1,0:T(8,128)(2,1)} %cand_hbm.1, bf16[1,2,3072,256]{3,2,1,0:T(8,128)(2,1)} %win_ref.1, bf16[1,2,256,3072]{3,2,1,0:T(8,128)(2,1)} %wout_ref.1), custom_call_target="tpu_custom_call" | custom-call | tf_op jit(solution)/shard_map/pallas_call | solution.py:726
  69.9 0.7 copy.9
  70.6 0.7 copy.10

commit v4 on v3

--- a/solution.py
+++ b/solution.py
@@ -105,6 +105,8 @@
     pieces = range(PIECES)
     pairs = ((c1 + 2 - 2 * path, c1 + 2 * path), (c2 + 2 * path, c2 + 2 - 2 * path))
 
+    spared = (core == 0) & (k == 0)
+
     def own(ph):
         return (ph + 1 + path) % 2
 
@@ -158,6 +160,23 @@
         def _():
             all_rows.start()
 
+    side, row, column = d // 16, (d // 4) % 4, d % 4
+    planes = [16 * ((side + 1) % 2), 16 * side]
+    columns = [(column + away) % 4 for away in (2, 1, 3, 0)]
+
+    def each_peer(do, too=0):
+        def line(n, carry):
+            at = 4 * ((row + (2 + 3 * (n * (n + 1) // 2)) % 4) % 4)
+            for x in columns:
+                for z in planes:
+                    do(z + at + x, at + x)
+            return carry
+
+        lax.fori_loop(0, 3, line, 0)
+        near = [(z, x) for x in columns for z in planes]
+        for z, x in near[: 7 + too]:
+            do(z + 4 * row + x, 4 * row + x)
+
     barrier = pltpu.get_barrier_semaphore()
 
     def hello(to):
@@ -173,23 +192,10 @@
     def _():
         hello(down)
 
-    def greet(n, carry):
-        pl.semaphore_signal(
-            barrier, inc=1, device_id={"dp": lax.rem(d + n, n_dp)}, device_id_type=MESH
-        )
-        return carry
-
-    lax.fori_loop(1, n_dp, greet, 0)
-
-    def far_first(n):
-        side = d // 16, (d // 4) % 4, d % 4
-
-        def away(t):
-            return (2 + 3 * (t * (t + 1) // 2)) % 4
-
-        plane = (side[0] + 1 - n % 2) % 2
-        column = (side[1] + away(n // 8)) % 4
-        return 16 * plane + 4 * column + (side[2] + away((n // 2) % 4)) % 4
+    def greet(peer, place):
+        pl.semaphore_signal(barrier, inc=1, device_id={"dp": peer}, device_id_type=MESH)
+
+    each_peer(greet)
 
     def piece_at(j):
         return pl.ds(j * piece, piece)
@@ -260,46 +266,59 @@
         ids_own[2:3, :] = target
         ids_all[d] = ids_own[...]
 
-        def send(n, carry):
+        def send(peer, place):
             pltpu.make_async_remote_copy(
                 src_ref=ids_own,
                 dst_ref=ids_all.at[d],
                 send_sem=ids_send,
                 recv_sem=ids_recv,
-                device_id={"dp": lax.rem(d + n, n_dp)},
+                device_id={"dp": peer},
                 device_id_type=MESH,
             ).start()
-            return carry
-
-        lax.fori_loop(1, n_dp, send, 0)
-
-    def spread(ph, narrow, broad):
+
+        each_peer(send)
+
+    def spread(ph, n, for_other=False):
         c, kind = cs[ph], ph // 2
+        box = 2 if for_other else c
+        narrow, broad = small.at[ph, n], xs.at[ph, n]
         narrow, broad = narrow[...], broad[...].astype(F32)
         hidden = narrow.shape[1] // 2
         top = jnp.concatenate([narrow[:, :hidden], narrow[:, hidden:]], axis=0).astype(BF16)
         wide = jnp.concatenate([broad, broad[:, :128]], axis=1)
         for j in range(half_dp):
-            sbuf[c, kind, j, 0:16, :] = top
-            sbuf[c, kind, j, 16:32, :] = wide[:, share * j : share * j + 128].astype(BF16)
-        rbuf[c, kind, d] = sbuf[c, kind, block]
-
-        def send(n, carry):
-            peer = far_first(n)
+            sbuf[box, kind, j, 0:16, :] = top
+            sbuf[box, kind, j, 16:32, :] = wide[:, share * j : share * j + 128].astype(BF16)
+
+        def send(peer, place):
             pltpu.make_async_remote_copy(
-                src_ref=sbuf.at[c, kind, lax.rem(peer, half_dp)],
+                src_ref=sbuf.at[box, kind, place],
                 dst_ref=rbuf.at[c, kind, d],
-                send_sem=x_send.at[c, kind],
+                send_sem=x_send.at[box, kind],
                 recv_sem=x_recv.at[c, kind],
-                device_id={"dp": peer},
+                device_id={"pipe": other, "dp": peer} if for_other else {"dp": peer},
                 device_id_type=MESH,
             ).start()
-            return carry
-
-        lax.fori_loop(0, n_dp - 1, send, 0)
-
-    def deliver(ph, n):
-        spread(ph, small.at[ph, n], xs.at[ph, n])
+
+        each_peer(send, 1 if for_other else 0)
+        if not for_other:
+            rbuf[c, kind, d] = sbuf[c, kind, block]
+
+    def all_here(c, kind):
+        def these(number):
+            many(rbuf.at[c, kind, pl.ds(0, number)], x_recv.at[c, kind]).wait()
+
+        if kind == 0:
+            these(n_dp - 1)
+        else:
+
+            @pl.when(spared & (c == c1))
+            def _():
+                these(n_dp)
+
+            @pl.when(jnp.logical_not(spared & (c == c1)))
+            def _():
+                these(n_dp - 1)
 
     def many(ref, sem):
         return pltpu.make_async_copy(ref, ref, sem)
@@ -325,7 +344,7 @@
                 sent(j)
 
     def activate(pre, w):
-        logistic = 1.0 / (1.0 + jnp.exp(-pre))
+        logistic = 0.5 + 0.5 * jnp.tanh(0.5 * pre)
         slopes[w] = logistic * (1.0 + pre * (1.0 - logistic))
         return pre * logistic
 
@@ -359,7 +378,6 @@
         small[ph, 1] = act_b
         parts = [(act_a, w_out, a), (twice(act_b), w_out, b)]
         add_branch(give.at[ph], xs.at[ph, 0], parts, sent)
-        return parts
 
     def backward_pair(ph, arrived):
         a, b = pairs[3 - ph]
@@ -395,7 +413,7 @@
         lax.fori_loop(0, 4 * (2 * half // tile), one, 0)
 
     def unpack(c, kind):
-        many(rbuf.at[c, kind, pl.ds(0, n_dp - 1)], x_recv.at[c, kind]).wait()
+        all_here(c, kind)
         rows = rbuf[c, kind].astype(F32)
         flat = lambda part: part.reshape(n_dp * 8, 128)
         narrow = jnp.concatenate([flat(rows[:, 0:8]), flat(rows[:, 8:16])], axis=1)
@@ -490,23 +508,22 @@
             for copy in mail(0):
                 copy.wait_recv()
 
-        deliver(0, 1 - own(0))
+        spread(0, 1 - own(0))
         for ph in (1, 2):
             for copy in mail(ph):
                 copy.wait_recv()
-            deliver(ph, 1 - own(ph))
+            spread(ph, 1 - own(ph))
         prepare()
 
         @pl.when(k == 0)
         def _():
             finish(early)
 
-        for copy in mail(3):
-            copy.wait_recv()
-        deliver(3, 1 - own(3))
-
         @pl.when(k > 0)
         def _():
+            for copy in mail(3):
+                copy.wait_recv()
+            spread(3, 1 - own(3))
             finish(early)
 
         finish(1 - early)
@@ -555,14 +572,24 @@
             for copy in lend((c1, c2)[blk]):
                 copy.wait_recv()
 
+        def middle(ph):
+            w = pairs[ph][0] if ph < 2 else pairs[3 - ph][1]
+            weights = w_out if ph < 2 else t_in
+            add_branch(xs.at[ph, 1], xs.at[ph, 0], [(twice(small[ph, 0]), weights, w)])
+
         def post(ph):
             for copy in mail(ph):
                 copy.start()
 
+        def settle(ph):
+            middle(ph)
+            post(ph)
+            spread(ph, own(ph))
+
         @pl.when(k == 0)
         def _():
             spread_ids()
-            deliver(0, own(0))
+            spread(0, own(0))
             lent(0)
             between(0)
             for copy in load(c2):
@@ -589,9 +616,7 @@
                 lent(1)
                 between(1)
 
-            parts = forward_pair(0, from_below(0), to_above(0))
-            add_branch(xs.at[0, 1], xs.at[0, 0], parts[:1])
-            post(0)
+            forward_pair(0, from_below(0), to_above(0))
 
             @pl.when(k == last)
             def _():
@@ -599,7 +624,7 @@
 
             @pl.when(k < last)
             def _():
-                deliver(0, own(0))
+                settle(0)
                 for copy in load(c2):
                     copy.wait()
                 lent(1)
@@ -609,17 +634,15 @@
                 def _():
                     turn()
 
-        parts = forward_pair(1, from_above(1), to_below(1))
-        add_branch(xs.at[1, 1], xs.at[1, 0], parts[:1])
-        post(1)
+        forward_pair(1, from_above(1), to_below(1))
 
         @pl.when(k > 0)
         def _():
-            deliver(1, own(1))
+            settle(1)
 
             @pl.when(k == last)
             def _():
-                deliver(0, own(0))
+                settle(0)
 
             @pl.when(k >= chips // 2)
             def _():
@@ -627,16 +650,14 @@
 
         parts = backward_pair(2, from_below(2))
         add_branch(give.at[2], xs.at[2, 0], parts, to_above(2))
-        add_branch(xs.at[2, 1], xs.at[2, 0], parts[:1])
-        post(2)
 
         @pl.when(k < last)
         def _():
             @pl.when(k == 0)
             def _():
-                deliver(1, own(1))
-
-            deliver(2, own(2))
+                settle(1)
+
+            settle(2)
             prepare()
 
             @pl.when(k == 0)
@@ -652,14 +673,25 @@
         @pl.when(k > 0)
         def _():
             add_branch(give.at[3], xs.at[3, 0], parts, to_below(3))
-
-        add_branch(xs.at[3, 1], xs.at[3, 0], parts[:1])
-        post(3)
-        deliver(3, own(3))
+            settle(3)
+
+        @pl.when(k == 0)
+        def _():
+            @pl.when(path == 0)
+            def _():
+                spread(3, 0)
+                middle(3)
+                spread(3, 1, True)
+
+            @pl.when(path == 1)
+            def _():
+                spread(3, 0, True)
+                middle(3)
+                spread(3, 1)
 
         @pl.when(k == last)
         def _():
-            deliver(2, own(2))
+            settle(2)
             prepare()
 
         @pl.when(k > 0)
@@ -683,13 +715,18 @@
             for j in pieces:
                 hop(1, j, down).wait_send()
                 hop(3, j, down).wait_send()
-            for copy in mail(0):
-                copy.wait_send()
-
-        for ph in (1, 2, 3):
+            for ph in (0, 3):
+                for copy in mail(ph):
+                    copy.wait_send()
+
+        for ph in (1, 2):
             for copy in mail(ph):
                 copy.wait_send()
 
+        @pl.when(k == 0)
+        def _():
+            many(rbuf.at[0, 0], x_send.at[2, 1]).wait()
+
         @pl.when(k == last)
         def _():
             many(ids_all.at[pl.ds(0, n_dp - 1)], ids_recv).wait()
@@ -709,9 +746,15 @@
             for j in pieces:
                 hop(0, j, up).wait_send()
 
-    for c in (0, 1):
-        for kind in (0, 1):
-            many(rbuf.at[c, kind, pl.ds(0, n_dp - 1)], x_send.at[c, kind]).wait()
+    def gone(c, kind):
+        many(rbuf.at[c, kind, pl.ds(0, n_dp - 1)], x_send.at[c, kind]).wait()
+
+    for ph in range(3):
+        gone(cs[ph], ph // 2)
+
+    @pl.when(jnp.logical_not(spared))
+    def _():
+        gone(cs[3], 1)
 
 
 def local(n_pipe, n_dp, item_ids, plan_order, candidates, adapters_in, adapters_out):
@@ -747,7 +790,7 @@
             pltpu.VMEM((4, 16, features // 2), BF16),
             pltpu.VMEM((4, 2, 8, hidden), F32),
             pltpu.VMEM((4, 8, hidden), F32),
-            pltpu.VMEM((2, 2, n_dp // 2, 32, 128), BF16),
+            pltpu.VMEM((3, 2, n_dp // 2, 32, 128), BF16),
             pltpu.VMEM((2, 2, n_dp, 32, 128), BF16),
             pltpu.VMEM((2, 128, n_dp * 8), BF16),
             pltpu.VMEM((2, n_dp * 8, hidden), BF16),
@@ -765,7 +808,7 @@
             pltpu.SemaphoreType.DMA,
             pltpu.SemaphoreType.DMA,
             pltpu.SemaphoreType.DMA,
-            pltpu.SemaphoreType.DMA((2, 2)),
+            pltpu.SemaphoreType.DMA((3, 2)),
             pltpu.SemaphoreType.DMA((2, 2)),
         ],
         compiler_params=pltpu.CompilerParams(

time: 71.6 us -> 69.5 us (0.971)
  Pallas kernels: 67.9 us -> 66 us
    pallas_call x1, Pallas kernels: 67.9 us -> 66 us  [local(): pl.pallas_call(functools.partial(kernel, n_pipe, n_dp, scale), out_shape=...]
where the time goes in v4:
time: 69.5 us; the launch traced here: 69.4 us
  Pallas kernels  66 us (95%)
  other arithmetic  1.41 us (2%)
  local copies, waits for them, and re-layouts  1.36 us (2%)
    pallas_call x1, Pallas kernels, local(): pl.pallas_call(functools.partial(kernel, n_pipe, n_dp, scale), out_shape=...  66 us

profile of v4, /device:TPU:32, one launch (start us, length us, event | category | flops | bytes accessed | tf_op | source)
XLA Modules:
  0.0 69.4 jit_solution(10315157324564378923)
XLA Ops:
  0.6 0.7 broadcast_multiply_fusion
  1.3 0.8 %broadcast_add_fusion.ids_hbm = s32[4,33]{1,0:T(4,128)S(1)} fusion(s32[4,33]{1,0:T(4,128)} %param.5, s32[4]{0:T(128)S(1)} %broadcast_multiply_fusion), kind=kLoop, calls=%fused_computation | loop fusion | flops 132 | bytes 1072 | tf_op jit(solution)/shard_map/add | solution.py:766
  2.0 66.0 %shard_map.68 = (f32[1,2,96,256]{3,2,1,0:T(8,128)S(1)}, f32[1,2,96,256]{3,2,1,0:T(8,128)S(1)}) custom-call(s32[4,33]{1,0:T(4,128)S(1)} %broadcast_add_fusion.ids_hbm, bf16[128,3072]{1,0:T(8,128)(2,1)} %cand_hbm.1, bf16[1,2,3072,256]{3,2,1,0:T(8,128)(2,1)} %win_ref.1, bf16[1,2,256,3072]{3,2,1,0:T(8,128)(2,1)} %wout_ref.1), custom_call_target="tpu_custom_call" | custom-call | tf_op jit(solution)/shard_map/pallas_call | solution.py:769
  68.1 0.7 copy.9
  68.7 0.7 copy.10

commit v5 on v4

--- a/solution.py
+++ b/solution.py
@@ -80,6 +80,7 @@
     ids_recv,
     x_send,
     x_recv,
+    met,
 ):
     p = lax.axis_index("pipe")
     d = lax.axis_index("dp")
@@ -192,10 +193,28 @@
     def _():
         hello(down)
 
-    def greet(peer, place):
-        pl.semaphore_signal(barrier, inc=1, device_id={"dp": peer}, device_id_type=MESH)
-
-    each_peer(greet)
+    beside = [16 * side + 4 * row + (column + step) % 4 for step in (1, 3)]
+    above = [16 * side + 4 * ((row + step) % 4) + column for step in (1, 3)]
+    facing = 16 * ((side + 1) % 2) + 4 * row + column
+
+    @pl.when(relay)
+    def _():
+        for peer in (*beside, *above, facing):
+            pl.semaphore_signal(barrier, inc=1, device_id={"dp": peer}, device_id_type=MESH)
+
+    def meet(n, peers):
+        for peer in peers:
+            pl.semaphore_signal(met.at[n], inc=1, device_id={"dp": peer}, device_id_type=MESH)
+
+    def meet_own_plane():
+        for n, peers in enumerate((beside, beside, above, above)):
+            meet(n, peers)
+            pl.semaphore_wait(met.at[n], 2)
+        meet(4, [facing])
+
+    def meet_other_plane():
+        pl.semaphore_wait(met.at[4], 1)
+        pl.semaphore_signal(met.at[5], inc=1, device_id={"pipe": other}, device_id_type=MESH)
 
     def piece_at(j):
         return pl.ds(j * piece, piece)
@@ -465,15 +484,15 @@
 
     @pl.when(relay & (k > 0) & (k < last))
     def _():
-        pl.semaphore_wait(barrier, n_dp + 2)
+        pl.semaphore_wait(barrier, 8)
 
     @pl.when(relay & edge)
     def _():
-        pl.semaphore_wait(barrier, n_dp + 1)
+        pl.semaphore_wait(barrier, 7)
 
     @pl.when(jnp.logical_not(relay))
     def _():
-        pl.semaphore_wait(barrier, n_dp)
+        pl.semaphore_wait(barrier, 1)
 
     @pl.when(k == 0)
     def _():
@@ -508,6 +527,7 @@
             for copy in mail(0):
                 copy.wait_recv()
 
+        pl.semaphore_wait(met.at[5], 1)
         spread(0, 1 - own(0))
         for ph in (1, 2):
             for copy in mail(ph):
@@ -588,6 +608,8 @@
 
         @pl.when(k == 0)
         def _():
+            meet_own_plane()
+            meet_other_plane()
             spread_ids()
             spread(0, own(0))
             lent(0)
@@ -603,6 +625,10 @@
 
         @pl.when(k > 0)
         def _():
+            @pl.when(k > 1)
+            def _():
+                meet_own_plane()
+
             for copy in load(c1):
                 copy.wait()
             lent(0)
@@ -610,6 +636,7 @@
 
             @pl.when(k == last)
             def _():
+                meet_other_plane()
                 spread_ids()
                 for copy in load(c2):
                     copy.wait()
@@ -622,8 +649,13 @@
             def _():
                 xs[1, 0] = give[0]
 
+            @pl.when(k == 1)
+            def _():
+                meet_own_plane()
+
             @pl.when(k < last)
             def _():
+                meet_other_plane()
                 settle(0)
                 for copy in load(c2):
                     copy.wait()
@@ -810,6 +842,7 @@
             pltpu.SemaphoreType.DMA,
             pltpu.SemaphoreType.DMA((3, 2)),
             pltpu.SemaphoreType.DMA((2, 2)),
+            pltpu.SemaphoreType.REGULAR((6,)),
         ],
         compiler_params=pltpu.CompilerParams(
             collective_id=0, has_side_effects=True, vmem_limit_bytes=107 * 512 * 1024

time: 69.5 us -> 66.7 us (0.960)
  Pallas kernels: 66 us -> 63.2 us
    pallas_call x1, Pallas kernels: 66 us -> 63.2 us  [local(): pl.pallas_call(functools.partial(kernel, n_pipe, n_dp, scale), out_shape=...]
where the time goes in v5:
time: 66.7 us; the launch traced here: 66.6 us
  Pallas kernels  63.2 us (95%)
  other arithmetic  1.41 us (2%)
  local copies, waits for them, and re-layouts  1.36 us (2%)
    pallas_call x1, Pallas kernels, local(): pl.pallas_call(functools.partial(kernel, n_pipe, n_dp, scale), out_shape=...  63.2 us
    unnamed x2, local copies, waits for them, and re-layouts  1.36 us

profile of v5, /device:TPU:32, one launch (start us, length us, event | category | flops | bytes accessed | tf_op | source)
XLA Modules:
  0.0 66.6 jit_solution(10351030892842737553)
XLA Ops:
  0.6 0.7 broadcast_multiply_fusion
  1.3 0.8 %broadcast_add_fusion.ids_hbm = s32[4,33]{1,0:T(4,128)S(1)} fusion(s32[4,33]{1,0:T(4,128)} %param.5, s32[4]{0:T(128)S(1)} %broadcast_multiply_fusion), kind=kLoop, calls=%fused_computation | loop fusion | flops 132 | bytes 1072 | tf_op jit(solution)/shard_map/add | solution.py:798
  2.0 63.2 %shard_map.68 = (f32[1,2,96,256]{3,2,1,0:T(8,128)S(1)}, f32[1,2,96,256]{3,2,1,0:T(8,128)S(1)}) custom-call(s32[4,33]{1,0:T(4,128)S(1)} %broadcast_add_fusion.ids_hbm, bf16[128,3072]{1,0:T(8,128)(2,1)} %cand_hbm.1, bf16[1,2,3072,256]{3,2,1,0:T(8,128)(2,1)} %win_ref.1, bf16[1,2,256,3072]{3,2,1,0:T(8,128)(2,1)} %wout_ref.1), custom_call_target="tpu_custom_call" | custom-call | tf_op jit(solution)/shard_map/pallas_call | solution.py:801
  65.2 0.7 %copy.9 = f32[1,2,96,256]{3,2,1,0:T(8,128)} copy(f32[1,2,96,256]{3,2,1,0:T(8,128)S(1)} %get-tuple-element.8) | data formatting | bytes 393216
  65.9 0.7 %copy.10 = f32[1,2,256,96]{2,3,1,0:T(8,128)} copy(f32[1,2,256,96]{2,3,1,0:T(8,128)S(1)} %bitcast.1) | data formatting | bytes 393216

commit v6 on v5

--- a/solution.py
+++ b/solution.py
@@ -60,6 +60,7 @@
     give,
     small,
     slopes,
+    bases,
     sbuf,
     rbuf,
     x_turned,
@@ -206,11 +207,11 @@
         for peer in peers:
             pl.semaphore_signal(met.at[n], inc=1, device_id={"dp": peer}, device_id_type=MESH)
 
-    def meet_own_plane():
-        for n, peers in enumerate((beside, beside, above, above)):
-            meet(n, peers)
-            pl.semaphore_wait(met.at[n], 2)
-        meet(4, [facing])
+    rounds = (beside, beside, above, above, [facing])
+
+    def met_by(n):
+        pl.semaphore_wait(met.at[n], 2)
+        meet(n + 1, rounds[n + 1])
 
     def meet_other_plane():
         pl.semaphore_wait(met.at[4], 1)
@@ -396,9 +397,16 @@
         act_b = activate(gather(sums_b) + mm(act_a, m_fwd[ph])[:8], b)
         small[ph, 1] = act_b
         parts = [(act_a, w_out, a), (twice(act_b), w_out, b)]
-        add_branch(give.at[ph], xs.at[ph, 0], parts, sent)
-
-    def backward_pair(ph, arrived):
+
+        def onward():
+            add_branch(give.at[ph], xs.at[ph, 0], parts, sent)
+
+        if ph == 0:
+            onward()
+        else:
+            pl.when(k > 0)(onward)
+
+    def backward_sums(ph, arrived):
         a, b = pairs[3 - ph]
         sums_a, sums_b = nothing(), nothing()
         for j in pieces:
@@ -406,10 +414,15 @@
             g2 = xs[ph, 0, :, piece_at(j)]
             sums_b = project(g2, j, t_out, b, sums_b)
             sums_a = project(g2, j, t_out, a, sums_a)
-        grad_b = gather(sums_b) * slopes[b]
+        bases[0] = gather(sums_a)
+        bases[1] = gather(sums_b)
+
+    def backward_pair(ph):
+        a, b = pairs[3 - ph]
+        grad_b = bases[1] * slopes[b]
         small[ph, 0] = grad_b
         grad_b = twice(grad_b)
-        grad_a = (gather(sums_a) + mm(grad_b, m_bwd[3 - ph])[:8]) * slopes[a]
+        grad_a = (bases[0] + mm(grad_b, m_bwd[3 - ph])[:8]) * slopes[a]
         small[ph, 1] = grad_a
         return [(grad_b, t_in, b), (twice(grad_a), t_in, a)]
 
@@ -419,17 +432,16 @@
         m_fwd[blk] = both.astype(BF16)
         m_bwd[blk] = both.T.astype(BF16)
 
-    def turn():
+    def turn(w):
         tile = w_in.shape[2]
 
         def one(n, carry):
-            w, at = n // (2 * half // tile), n % (2 * half // tile)
-            at = pl.ds(pl.multiple_of(at * tile, tile), tile)
+            at = pl.ds(pl.multiple_of(n * tile, tile), tile)
             t_in[w, :, at] = w_in[w, at, :].T
             t_out[w, at, :] = w_out[w, :, at].T
             return carry
 
-        lax.fori_loop(0, 4 * (2 * half // tile), one, 0)
+        lax.fori_loop(0, 2 * half // tile, one, 0)
 
     def unpack(c, kind):
         all_here(c, kind)
@@ -606,40 +618,58 @@
             post(ph)
             spread(ph, own(ph))
 
+        def ready(blk):
+            for copy in load((c1, c2)[blk]):
+                copy.wait()
+
+        def turn_and_meet():
+            turn(c1)
+            met_by(0)
+            ready(1)
+            turn(c2)
+            met_by(1)
+
+            @pl.when(k == 0)
+            def _():
+                lent(0)
+
+            turn(2 + c1)
+            met_by(2)
+            lent(1)
+            turn(2 + c2)
+            met_by(3)
+
         @pl.when(k == 0)
         def _():
-            meet_own_plane()
+            meet(0, rounds[0])
+            turn_and_meet()
             meet_other_plane()
             spread_ids()
             spread(0, own(0))
+            between(0)
+            between(1)
+            many(ids_all.at[pl.ds(0, n_dp - 1)], ids_recv).wait()
+            seeds()
+            backward_sums(2, lambda j: None)
+            back().wait_recv()
+
+        @pl.when(k > 0)
+        def _():
+            meet(0, rounds[0])
+            ready(0)
             lent(0)
             between(0)
-            for copy in load(c2):
-                copy.wait()
-            lent(1)
-            between(1)
-            turn()
-            many(ids_all.at[pl.ds(0, n_dp - 1)], ids_recv).wait()
-            seeds()
-            back().wait_recv()
-
-        @pl.when(k > 0)
-        def _():
+
             @pl.when(k > 1)
             def _():
-                meet_own_plane()
-
-            for copy in load(c1):
-                copy.wait()
-            lent(0)
-            between(0)
+                met_by(0)
 
             @pl.when(k == last)
             def _():
-                meet_other_plane()
-                spread_ids()
-                for copy in load(c2):
-                    copy.wait()
+                met_by(1)
+                met_by(2)
+                met_by(3)
+                ready(1)
                 lent(1)
                 between(1)
 
@@ -651,36 +681,45 @@
 
             @pl.when(k == 1)
             def _():
-                meet_own_plane()
-
-            @pl.when(k < last)
-            def _():
+                turn_and_meet()
+                between(1)
                 meet_other_plane()
                 settle(0)
-                for copy in load(c2):
-                    copy.wait()
+
+            @pl.when((k > 1) & (k < last))
+            def _():
+                met_by(1)
+                met_by(2)
+                met_by(3)
+                ready(1)
                 lent(1)
                 between(1)
 
-                @pl.when(k < chips // 2)
+        forward_pair(1, from_above(1), to_below(1))
+
+        @pl.when(k > 0)
+        def _():
+            @pl.when(k > 1)
+            def _():
+                meet_other_plane()
+
+                @pl.when(k == last)
                 def _():
-                    turn()
-
-        forward_pair(1, from_above(1), to_below(1))
+                    spread_ids()
+
+            settle(1)
+
+            @pl.when(k > 1)
+            def _():
+                settle(0)
+                for w in range(4):
+                    turn(w)
 
         @pl.when(k > 0)
         def _():
-            settle(1)
-
-            @pl.when(k == last)
-            def _():
-                settle(0)
-
-            @pl.when(k >= chips // 2)
-            def _():
-                turn()
-
-        parts = backward_pair(2, from_below(2))
+            backward_sums(2, lambda j: hop(2, j, down).wait_recv())
+
+        parts = backward_pair(2)
         add_branch(give.at[2], xs.at[2, 0], parts, to_above(2))
 
         @pl.when(k < last)
@@ -700,7 +739,8 @@
         def _():
             xs[3, 0] = give[2]
 
-        parts = backward_pair(3, from_above(3))
+        backward_sums(3, from_above(3))
+        parts = backward_pair(3)
 
         @pl.when(k > 0)
         def _():
@@ -822,6 +862,7 @@
             pltpu.VMEM((4, 16, features // 2), BF16),
             pltpu.VMEM((4, 2, 8, hidden), F32),
             pltpu.VMEM((4, 8, hidden), F32),
+            pltpu.VMEM((2, 8, hidden), F32),
             pltpu.VMEM((3, 2, n_dp // 2, 32, 128), BF16),
             pltpu.VMEM((2, 2, n_dp, 32, 128), BF16),
             pltpu.VMEM((2, 128, n_dp * 8), BF16),

time: 66.7 us -> 66.3 us (level)
  no operation moved by 1% of the time
where the time goes in v6:
time: 66.3 us; the launch traced here: 66.2 us
  Pallas kernels  62.8 us (95%)
  other arithmetic  1.41 us (2%)
  local copies, waits for them, and re-layouts  1.36 us (2%)
    pallas_call x1, Pallas kernels, local(): pl.pallas_call(functools.partial(kernel, n_pipe, n_dp, scale), out_shape=...  62.8 us
    unnamed x2, local copies, waits for them, and re-layouts  1.36 us

profile of v6, /device:TPU:32, one launch (start us, length us, event | category | flops | bytes accessed | tf_op | source)
XLA Modules:
  0.0 66.2 jit_solution(16779052730455806582)
XLA Ops:
  0.6 0.7 broadcast_multiply_fusion
  1.3 0.8 %broadcast_add_fusion.ids_hbm = s32[4,33]{1,0:T(4,128)S(1)} fusion(s32[4,33]{1,0:T(4,128)} %param.5, s32[4]{0:T(128)S(1)} %broadcast_multiply_fusion), kind=kLoop, calls=%fused_computation | loop fusion | flops 132 | bytes 1072 | tf_op jit(solution)/shard_map/add | solution.py:838
  2.0 62.8 %shard_map.68 = (f32[1,2,96,256]{3,2,1,0:T(8,128)S(1)}, f32[1,2,96,256]{3,2,1,0:T(8,128)S(1)}) custom-call(s32[4,33]{1,0:T(4,128)S(1)} %broadcast_add_fusion.ids_hbm, bf16[128,3072]{1,0:T(8,128)(2,1)} %cand_hbm.1, bf16[1,2,3072,256]{3,2,1,0:T(8,128)(2,1)} %win_ref.1, bf16[1,2,256,3072]{3,2,1,0:T(8,128)(2,1)} %wout_ref.1), custom_call_target="tpu_custom_call" | custom-call | tf_op jit(solution)/shard_map/pallas_call | solution.py:841
  64.8 0.7 %copy.9 = f32[1,2,96,256]{3,2,1,0:T(8,128)} copy(f32[1,2,96,256]{3,2,1,0:T(8,128)S(1)} %get-tuple-element.8) | data formatting | bytes 393216
  65.5 0.7 %copy.10 = f32[1,2,256,96]{2,3,1,0:T(8,128)} copy(f32[1,2,256,96]{2,3,1,0:T(8,128)S(1)} %bitcast.1) | data formatting | bytes 393216

commit v7 on v6

--- a/solution.py
+++ b/solution.py
@@ -102,7 +102,6 @@
     down = 2 * chip - 1 + 4 * path
     edge = (k == 0) | (k == last)
     half = w_in.shape[1] // 2
-    n_items = cand_ref.shape[0]
     piece = half // PIECES
     pieces = range(PIECES)
     pairs = ((c1 + 2 - 2 * path, c1 + 2 * path), (c2 + 2 * path, c2 + 2 - 2 * path))
@@ -269,12 +268,11 @@
         lane = lax.broadcasted_iota(jnp.int32, (1, 128), 1)
         front = back = target = jnp.full((1, 128), -1, jnp.int32)
         ids_own[...] = jnp.full((8, 128), -1, jnp.int32)
-        ids_own[0:4, 0:33] = ids_ref[...]
+        ids_own[0:5, 0:33] = ids_ref[...]
+        plan = ids_own[4:5, :]
         for m in range(4):
             row = ids_own[m : m + 1, :]
-            is_front = row < 2 * n_items
-            for above in (2 * n_items, n_items):
-                row = jnp.where(row >= above, row - above, row)
+            is_front = plan[:, m : m + 1] < 2
             fronts = jnp.where(is_front, row, -1)
             backs = jnp.where(is_front, -1, row)
             here = lane // 32 == m
@@ -835,7 +833,10 @@
     _, _, features, hidden = adapters_in.shape
     share = features // n_dp
     scale = 1.0 / math.sqrt(batches * n_dp * events)
-    ids = item_ids + candidates.shape[0] * plan_order[:, None]
+    spare = width - plan_order.shape[0]
+    ids = lax.pad(item_ids, 0, ((0, 1, 0), (0, 0, 0))) + lax.pad(
+        plan_order[None, :], 0, ((batches, 0, 0), (0, spare, 0))
+    )
     vmem = pl.BlockSpec(memory_space=pltpu.VMEM)
     hbm = pl.BlockSpec(memory_space=pltpu.HBM)
     grad_in, grad_out = pl.pallas_call(

time: 66.3 us -> 65.7 us (level)
  other arithmetic: 1.41 us -> 0.71 us
where the time goes in v7:
time: 65.7 us; the launch traced here: 65.6 us
  Pallas kernels  62.9 us (96%)
  local copies, waits for them, and re-layouts  1.36 us (2%)
  other arithmetic  0.71 us (1%)
    pallas_call x1, Pallas kernels, local(): pl.pallas_call(functools.partial(kernel, n_pipe, n_dp, scale), out_shape=...  62.9 us
    unnamed x2, local copies, waits for them, and re-layouts  1.36 us

profile of v7, /device:TPU:32, one launch (start us, length us, event | category | flops | bytes accessed | tf_op | source)
XLA Modules:
  0.0 65.6 jit_solution(818184298366388801)
XLA Ops:
  0.6 0.7 %pad_add_fusion.ids_hbm = s32[5,33]{1,0:T(8,128)S(1)} fusion(s32[1,4]{1,0:T(1,128)} %bitcast.3, s32[4,33]{1,0:T(4,128)} %param.5), kind=kLoop, calls=%fused_computation | loop fusion | flops 165 | bytes 1204 | tf_op jit(solution)/shard_map/add | solution.py:837
  1.3 62.9 %shard_map.68 = (f32[1,2,96,256]{3,2,1,0:T(8,128)S(1)}, f32[1,2,96,256]{3,2,1,0:T(8,128)S(1)}) custom-call(s32[5,33]{1,0:T(8,128)S(1)} %pad_add_fusion.ids_hbm, bf16[128,3072]{1,0:T(8,128)(2,1)} %cand_hbm.1, bf16[1,2,3072,256]{3,2,1,0:T(8,128)(2,1)} %win_ref.1, bf16[1,2,256,3072]{3,2,1,0:T(8,128)(2,1)} %wout_ref.1), custom_call_target="tpu_custom_call" | custom-call | tf_op jit(solution)/shard_map/pallas_call | solution.py:842
  64.2 0.7 %copy.9 = f32[1,2,96,256]{3,2,1,0:T(8,128)} copy(f32[1,2,96,256]{3,2,1,0:T(8,128)S(1)} %get-tuple-element.8) | data formatting | bytes 393216
  64.9 0.7 %copy.10 = f32[1,2,256,96]{2,3,1,0:T(8,128)} copy(f32[1,2,256,96]{2,3,1,0:T(8,128)S(1)} %bitcast.2) | data formatting | bytes 393216

commit v8 on v7

--- a/solution.py
+++ b/solution.py
@@ -154,13 +154,6 @@
         def _():
             id_copy.start()
 
-        for copy in load(c2):
-            copy.start()
-
-        @pl.when(k == 0)
-        def _():
-            all_rows.start()
-
     side, row, column = d // 16, (d // 4) % 4, d % 4
     planes = [16 * ((side + 1) % 2), 16 * side]
     columns = [(column + away) % 4 for away in (2, 1, 3, 0)]
@@ -491,6 +484,15 @@
         for copy in load(c1):
             copy.wait()
         add_branch(xs.at[0, 1], xs.at[0, 0], forward_one(0))
+
+    @pl.when(relay)
+    def _():
+        for copy in load(c2):
+            copy.start()
+
+        @pl.when(k == 0)
+        def _():
+            all_rows.start()
 
     @pl.when(relay & (k > 0) & (k < last))
     def _():

time: 65.7 us -> 65.7 us (level)
  no operation moved by 1% of the time
where the time goes in v8:
time: 65.7 us; the launch traced here: 65.6 us
  Pallas kernels  62.9 us (96%)
  local copies, waits for them, and re-layouts  1.36 us (2%)
  other arithmetic  0.71 us (1%)
    pallas_call x1, Pallas kernels, local(): pl.pallas_call(functools.partial(kernel, n_pipe, n_dp, scale), out_shape=...  62.9 us
    unnamed x2, local copies, waits for them, and re-layouts  1.36 us

profile of v8, /device:TPU:32, one launch (start us, length us, event | category | flops | bytes accessed | tf_op | source)
XLA Modules:
  0.0 65.6 jit_solution(3141302413947842038)
XLA Ops:
  0.6 0.7 %pad_add_fusion.ids_hbm = s32[5,33]{1,0:T(8,128)S(1)} fusion(s32[1,4]{1,0:T(1,128)} %bitcast.3, s32[4,33]{1,0:T(4,128)} %param.5), kind=kLoop, calls=%fused_computation | loop fusion | flops 165 | bytes 1204 | tf_op jit(solution)/shard_map/add | solution.py:839
  1.3 62.9 %shard_map.68 = (f32[1,2,96,256]{3,2,1,0:T(8,128)S(1)}, f32[1,2,96,256]{3,2,1,0:T(8,128)S(1)}) custom-call(s32[5,33]{1,0:T(8,128)S(1)} %pad_add_fusion.ids_hbm, bf16[128,3072]{1,0:T(8,128)(2,1)} %cand_hbm.1, bf16[1,2,3072,256]{3,2,1,0:T(8,128)(2,1)} %win_ref.1, bf16[1,2,256,3072]{3,2,1,0:T(8,128)(2,1)} %wout_ref.1), custom_call_target="tpu_custom_call" | custom-call | tf_op jit(solution)/shard_map/pallas_call | solution.py:844
  64.2 0.7 %copy.9 = f32[1,2,96,256]{3,2,1,0:T(8,128)} copy(f32[1,2,96,256]{3,2,1,0:T(8,128)S(1)} %get-tuple-element.8) | data formatting | bytes 393216
  64.9 0.7 %copy.10 = f32[1,2,256,96]{2,3,1,0:T(8,128)} copy(f32[1,2,256,96]{2,3,1,0:T(8,128)S(1)} %bitcast.2) | data formatting | bytes 393216
